TPU v7x, 512 devices: a whole 4x4x16 slice. The times are simulated.
512 devices in a mesh: dp: 64 (over z, y), enc: 8 (over x, core).
Axes of the slice: x: 4, y: 4, z: 16, core: 2. Of those that a mesh axis runs over, the one named last changes fastest.
Arguments:
- tile_features: bfloat16 [4096, 4, 2, 3072], P('dp', None, None, 'enc'), may hold values from -6 to 6
- dw_kernel: float32 [49, 3072], P(None, 'enc'), may hold values from -0.875 to 0.875
- dw_bias: float32 [3072], P('enc'), may hold values from -3 to 3
- ln_gain: float32 [3072], P('enc'), may hold values from 0.1 to 1.9
- ln_shift: float32 [3072], P('enc'), may hold values from -3 to 3
- layer_scale: float32 [3072], P('enc'), may hold values from 0.3 to 3
- sample_counts: int32 [64, 8], P('dp'), may hold values from 1 to 16, 64 in all within a row
- tile_dest: int32 [64, 64], P('dp'), may hold values from 0 to 63, as said below
- tile_offset: int32 [64, 64], P('dp'), may hold values from 0 to 127, as said below
- seq_grad: bfloat16 [65536, 3072], P('dp', 'enc'), may hold values from -6 to 6
Outputs:
- visual_sequence: bfloat16 [65536, 3072], P('dp', 'enc')
- tile_grads: bfloat16 [4096, 4, 2, 3072], P('dp', None, None, 'enc')
- param_grads: float32 [53, 3072], P(None, 'enc')
Inputs may be any that keep to these rules, and one draw needn't show every extreme that they name: `tile_dest`: among one owner's tiles each shard is named at most 2 times; in every draw some shard is named exactly 2 times by every owner, so its 128 blocks are all used. `tile_offset`: tiles sent to one shard have distinct blocks. `sample_counts`: the counts of one owner sum to 64; the largest is 16.
All inputs are finite; a program needn't handle non-finite values.
Results may differ from a plain program's by a relative error of at most 0.00105.
Values may be sent and summed in bfloat16 or wider, within the bound.
No kernel may reach another device: no remote copies, remote signals or barrier semaphores. Data moves between devices by JAX's collectives and lax.ppermute only.
A program may use at most 64 MiB of HBM per device.

v0:
```python
import jax
import jax.numpy as jnp
from jax import lax
from jax.sharding import PartitionSpec as P

EPS = 1e-06


def conv_apply(tiles, kernel):
    hgt, wid = (tiles.shape[1], tiles.shape[2])
    padded = jnp.pad(tiles, ((0, 0), (3, 3), (3, 3), (0, 0)))
    total = jnp.zeros(tiles.shape, jnp.float32)
    for row in range(7):
        for col in range(7):
            total = total + kernel[row * 7 + col] * padded[
                :, row : row + hgt, col : col + wid, :
            ].astype(jnp.float32)
    return total


def forward_block(tiles, params, width):
    kernel, bias, gain, shift, scale = params
    filtered = conv_apply(tiles, kernel) + bias
    sums = lax.psum((jnp.sum(filtered, -1), jnp.sum(filtered * filtered, -1)), "enc")
    center = sums[0] / width
    inv = lax.rsqrt(sums[1] / width - center * center + EPS)[..., None]
    normed = (filtered - center[..., None]) * inv
    mixed = normed * gain + shift
    tokens = (tiles.astype(jnp.float32) + scale * mixed).astype(jnp.bfloat16)
    return (tokens, normed, mixed, inv)


def backward_block(tiles, normed, mixed, inv, upstream, params, width):
    kernel, bias, gain, shift, scale = params
    hgt, wid = (tiles.shape[1], tiles.shape[2])
    dscale = jnp.sum(upstream * mixed, (0, 1, 2))
    dshift = jnp.sum(upstream, (0, 1, 2)) * scale
    dgain = jnp.sum(upstream * normed, (0, 1, 2)) * scale
    dnormed = upstream * (scale * gain)
    sums = lax.psum((jnp.sum(dnormed, -1), jnp.sum(dnormed * normed, -1)), "enc")
    dfilt = inv * (dnormed - sums[0][..., None] / width - normed * (sums[1][..., None] / width))
    dbias = jnp.sum(dfilt, (0, 1, 2))
    padded_in = jnp.pad(tiles, ((0, 0), (3, 3), (3, 3), (0, 0)))
    padded_grad = jnp.pad(dfilt, ((0, 0), (3, 3), (3, 3), (0, 0)))
    taps = []
    dtiles = upstream
    for row in range(7):
        for col in range(7):
            shifted = padded_in[:, row : row + hgt, col : col + wid, :].astype(jnp.float32)
            taps.append(jnp.sum(dfilt * shifted, (0, 1, 2)))
            back = padded_grad[:, 6 - row : 6 - row + hgt, 6 - col : 6 - col + wid, :]
            dtiles = dtiles + kernel[row * 7 + col] * back
    grads = jnp.concatenate([jnp.stack(taps, 0), jnp.stack([dbias, dgain, dshift, dscale], 0)], 0)
    return (dtiles, grads)


def per_device(
    tile_features,
    dw_kernel,
    dw_bias,
    ln_gain,
    ln_shift,
    layer_scale,
    sample_counts,
    tile_dest,
    tile_offset,
    seq_grad,
):
    tiles_dev, hgt, wid, chans = tile_features.shape
    width = chans * lax.axis_size("enc")
    peers = lax.axis_size("dp")
    cap = tiles_dev // peers + 1
    slots = peers * cap
    blocks = peers * cap
    params = (dw_kernel, dw_bias, ln_gain, ln_shift, layer_scale)
    counts = sample_counts[0]
    dest = tile_dest[0]
    offsets = tile_offset[0]
    ends = jnp.cumsum(counts)
    sample = jnp.sum(
        (jnp.arange(tiles_dev, dtype=jnp.int32)[:, None] >= ends[None, :]).astype(jnp.int32), 1
    )
    member = sample[:, None] == jnp.arange(counts.shape[0], dtype=jnp.int32)[None, :]
    tile_count = jnp.sum(jnp.where(member, counts[None, :], 0), 1)
    picks = (dest[:, None] == jnp.arange(peers, dtype=jnp.int32)[None, :]).astype(jnp.int32)
    rank = jnp.sum((jnp.cumsum(picks, 0) - 1) * picks, 1)
    slot = dest * cap + rank
    grad_blocks = seq_grad.reshape(blocks, hgt, wid, chans)
    empty = jnp.zeros((slots, hgt, wid, chans), jnp.bfloat16)
    placed = jnp.zeros((blocks, hgt, wid, chans), jnp.bfloat16)
    send_tiles = empty.at[slot].set(tile_features).reshape(peers, cap, hgt, wid, chans)
    blank = jnp.stack([jnp.full((slots,), blocks, jnp.int32), jnp.zeros((slots,), jnp.int32)], 1)
    send_meta = blank.at[slot].set(jnp.stack([offsets, tile_count], 1)).reshape(peers, cap, 2)
    got_tiles, got_meta = (
        lax.all_to_all(send_tiles, "dp", split_axis=0, concat_axis=0, tiled=True),
        lax.all_to_all(send_meta, "dp", split_axis=0, concat_axis=0, tiled=True),
    )
    got_tiles = got_tiles.reshape(slots, hgt, wid, chans)
    flat_off = got_meta[..., 0].reshape(slots)
    got_count = got_meta[..., 1].reshape(slots)
    weight = jnp.where(got_count > 0, 8.0 / jnp.maximum(got_count, 1).astype(jnp.float32), 0.0)
    tokens, normed, mixed, inv = forward_block(got_tiles, params, width)
    placed = placed.at[flat_off].set(tokens, mode="drop")
    rows = grad_blocks[jnp.minimum(flat_off, blocks - 1)]
    upstream = rows.astype(jnp.float32) * weight[:, None, None, None]
    dtiles, grads = backward_block(got_tiles, normed, mixed, inv, upstream, params, width)
    outgoing = dtiles.astype(jnp.bfloat16).reshape(peers, cap, hgt, wid, chans)
    back = lax.all_to_all(outgoing, "dp", split_axis=0, concat_axis=0, tiled=True)
    tile_grads = back.reshape(slots, hgt, wid, chans)[slot]
    param_grads = lax.psum(grads, "dp")
    return (placed.reshape(blocks * hgt * wid, chans), tile_grads, param_grads)


def solution(mesh):
    placed = (
        P("dp", None, None, "enc"),
        P(None, "enc"),
        P("enc"),
        P("enc"),
        P("enc"),
        P("enc"),
        P("dp", None),
        P("dp", None),
        P("dp", None),
        P("dp", "enc"),
    )
    return jax.shard_map(
        per_device,
        mesh=mesh,
        in_specs=placed,
        out_specs=(P("dp", "enc"), P("dp", None, None, "enc"), P(None, "enc")),
        check_vma=False,
    )
```

profile of v0, /device:TPU:4, one launch (start us, length us, event | category | flops | bytes accessed | tf_op | source)
XLA Modules:
  0.0 486.8 jit_solution(15818735973769881213)
XLA Ops:
  7.2 0.7 fusion.103
  8.0 0.8 select_reduce_fusion
  8.8 0.7 fusion.104
  9.5 0.8 copy.46
  10.3 0.8 reduce-window.8
  11.3 0.7 select_reduce_fusion.1
  12.0 0.7 pad_add_fusion
  12.8 0.8 scatter_fusion
  13.6 1.1 copy.34
  14.7 18.7 %all-to-all-start = ((s32[64,2,2]{1,2,0:T(2,128)}), s32[64,2,2]{1,2,0:T(2,128)S(1)}, u32[]{:S(2)}, u32[]{:S(2)}) async-start(s32[64,2,2]{1,2,0:T(2,128)} %copy.34), calls=%async_computation | async-start | bytes 131072 | tf_op jit(solution)/shard_map/all_to_all | solution.py:96
  33.4 1.2 copy.35
  34.6 1.1 broadcast.383.clone
  35.6 8.0 %scatter_fusion.1 = bf16[128,4,2,384]{3,1,2,0:T(4,128)(2,1)} fusion(bf16[128,4,2,384]{3,1,2,0:T(4,128)(2,1)} %broadcast.383.clone, s32[64]{0:T(128)S(1)} %fusion.104, bf16[64,4,2,384]{3,1,2,0:T(4,128)(2,1)S(1)} %copy.35), kind=kCustom, calls=%fused_computation.3 | custom fusion | bytes 1179904 | tf_op jit(solution)/shard_map/scatter | solution.py:91
  43.6 5.0 %all-to-all-done = s32[64,2,2]{1,2,0:T(2,128)S(1)} async-done(((s32[64,2,2]{1,2,0:T(2,128)}), s32[64,2,2]{1,2,0:T(2,128)S(1)}, u32[]{:S(2)}, u32[]{:S(2)}) %all-to-all-start) | async-done | bytes 1056 | tf_op jit(solution)/shard_map/all_to_all | solution.py:96
  48.6 10.1 %all-to-all-start.1 = ((bf16[64,2,4,2,384]{4,2,3,1,0:T(4,128)(2,1)}), bf16[64,2,4,2,384]{4,2,3,1,0:T(4,128)(2,1)S(1)}, u32[]{:S(2)}, u32[]{:S(2)}) async-start(bf16[64,2,4,2,384]{4,2,3,1,0:T(4,128)(2,1)} %bitcast.11), calls=%async_computation.1 | async-start | bytes 1572864 | tf_op jit(solution)/shard_map/all_to_all | solution.py:95
  58.8 0.3 reshape.271
  59.1 0.3 copy.37
  59.4 0.2 copy-done.4
  59.9 0.1 multiply_reduce_fusion.31
  60.2 0.7 slice_reduce_fusion.21
  61.0 0.1 reshape_squeeze.4
  61.1 0.2 fusion.102
  61.3 0.7 select_n.52
  62.0 0.6 fusion.106
  62.6 1.3 gather_fusion
  63.9 38.3 %all-to-all-done.1 = bf16[64,2,4,2,384]{4,2,3,1,0:T(4,128)(2,1)S(1)} async-done(((bf16[64,2,4,2,384]{4,2,3,1,0:T(4,128)(2,1)}), bf16[64,2,4,2,384]{4,2,3,1,0:T(4,128)(2,1)S(1)}, u32[]{:S(2)}, u32[]{:S(2)}) %all-to-all-start.1) | async-done | bytes 786464 | tf_op jit(solution)/shard_map/all_to_all | solution.py:95
  102.6 11.8 %fusion.52 = f32[128,4,2,384]{3,1,2,0:T(4,128)S(1)} fusion(f32[384]{0:T(512)S(1)} %copy-done.108, f32[384]{0:T(512)} %get-tuple-element.94, f32[384]{0:T(512)} %get-tuple-element.95, f32[384]{0:T(512)S(1)} %get-tuple-element.48, f32[384]{0:T(512)S(1)} %get-tuple-element.49, f32[384]{0:T(512)S(1)} %get-tuple-element.50, f32[384]{0:T(512)S(1)} %get-tuple-element.51, ...), kind=kLoop, calls=%fused_computation.140 | loop fusion | flops 35389440 | bytes 3220992 | tf_op jit(solution)/shard_map/add | solution.py:23
  114.4 0.9 fusion.108
  115.3 22.6 %all-reduce.3 = (f32[128,4,2]{1,2,0:T(2,128)S(1)}, f32[128,4,2]{1,2,0:T(2,128)}) all-reduce(f32[128,4,2]{1,2,0:T(2,128)S(1)} %get-tuple-element.44, f32[128,4,2]{1,2,0:T(2,128)S(1)} %get-tuple-element.43), channel_id=1, replica_groups=mesh['dp'=64,'enc'=8] {'enc'}, use_global_device_ids=true, to_apply=%region_10.11 | all-reduce | flops 2048 | bytes 16384 | tf_op jit(solution)/shard_map/psum | solution.py:24
  137.9 1.1 broadcast_multiply_fusion.2
  139.0 7.4 %multiply_reduce_fusion = (f32[384]{0:T(512)}, f32[128,4,2]{1,2,0:T(2,128)S(1)}, f32[384]{0:T(512)}, f32[128,4,2]{1,2,0:T(2,128)}, f32[384]{0:T(512)}, /*index=5*/bf16[128,4,2,384]{3,1,2,0:T(4,128)(2,1)}) fusion(bf16[128,4,2,384]{3,1,2,0:T(4,128)(2,1)S(1)} %gather_fusion, f32[128]{0:T(128)} %select_n.52, f32[384]{0:T(512)} %param.14, f32[384]{0:T(512)} %param.13, ...), kind=kLoop, calls=%fused_computation.187 | loop fusion | flops 7467904 | bytes 3959808 | tf_op jit(solution)/shard_map/reduce_sum | solution.py:36
  146.4 26.0 %all-reduce.2 = (f32[128,4,2]{1,2,0:T(2,128)}, f32[128,4,2]{1,2,0:T(2,128)}) all-reduce(f32[128,4,2]{1,2,0:T(2,128)S(1)} %get-tuple-element.16, f32[128,4,2]{1,2,0:T(2,128)} %get-tuple-element.45), channel_id=1, replica_groups=mesh['dp'=64,'enc'=8] {'enc'}, use_global_device_ids=true, to_apply=%region_15.16 | all-reduce | flops 2048 | bytes 16384 | tf_op jit(solution)/shard_map/psum | solution.py:40
  172.4 1.1 broadcast_multiply_fusion
  173.9 11.7 %fusion.55 = (f32[384]{0:T(512)}, f32[384]{0:T(512)}, f32[384]{0:T(512)}, f32[384]{0:T(512)}, f32[384]{0:T(512)}, /*index=5*/f32[384]{0:T(512)}, f32[384]{0:T(51...) fusion(bf16[128,4,2,384]{3,1,2,0:T(4,128)(2,1)S(1)} %bitcast.27, ...), kind=kLoop, calls=%fused_computation.143 | loop fusion | flops 24765696 | bytes 4764672 | tf_op jit(solution)/shard_map/reduce_sum | solution.py:50
  186.0 13.1 %add_convert_fusion = bf16[128,4,2,384]{3,1,2,0:T(4,128)(2,1)} fusion(f32[128,4,2,384]{3,1,2,0:T(4,128)S(1)} %get-tuple-element.100, bf16[128,4,2,384]{3,1,2,0:T(4,128)(2,1)S(1)} %gather_fusion, f32[384]{0:T(512)S(1)} %get-tuple-element.47, f32[384]{0:T(512)S(1)} %get-tuple-element.66, f32[128]{0:T(128)S(1)} %copy-done.87, f32[384]{0:T(512)} %get-tuple-element.94, ...), kind=kLoop, calls=%fused_computation.190 | loop fusion | flops 28704768 | bytes 3221504 | tf_op jit(solution)/shard_map/convert_element_type | solution.py:107
  199.0 7.2 %all-to-all-start.2 = ((bf16[64,2,4,2,384]{4,2,3,1,0:T(4,128)(2,1)}), bf16[64,2,4,2,384]{4,2,3,1,0:T(4,128)(2,1)}, u32[]{:S(2)}, u32[]{:S(2)}) async-start(bf16[64,2,4,2,384]{4,2,3,1,0:T(4,128)(2,1)} %bitcast.29), calls=%async_computation.2 | async-start | bytes 1572864 | tf_op jit(solution)/shard_map/all_to_all | solution.py:108
  206.3 0.7 fusion.109
  207.2 2.3 fusion.107
  210.0 4.4 concatenate.3
  214.4 0.2 broadcast.383
  214.6 4.8 scatter_fusion.2
  219.4 0.6 copy.36
  220.0 1.2 reshape.270
  221.2 30.0 %all-to-all-done.2 = bf16[64,2,4,2,384]{4,2,3,1,0:T(4,128)(2,1)} async-done(((bf16[64,2,4,2,384]{4,2,3,1,0:T(4,128)(2,1)}), bf16[64,2,4,2,384]{4,2,3,1,0:T(4,128)(2,1)}, u32[]{:S(2)}, u32[]{:S(2)}) %all-to-all-start.2) | async-done | bytes 786464 | tf_op jit(solution)/shard_map/all_to_all | solution.py:108
  251.2 2.1 gather_fusion.1
  253.3 1.1 copy.38
  254.3 224.1 %all-reduce.6.cloned.1.call-done = f32[53,384]{1,0:T(8,128)} async-done(((f32[53,384]{1,0:T(8,128)}), f32[53,384]{1,0:T(8,128)}) %all-reduce.6.cloned.1.call-update) | async-done | bytes 81424 | tf_op jit(solution)/shard_map/psum | solution.py:110
  478.4 1.5 copy.47
  (256 shorter events, 1.1 us)
Async XLA Ops:
  9.5 34.1 %copy-start.106 = (s32[64]{0:T(128)}, s32[64]{0:T(128)S(1)}, u32[]{:S(2)}) copy-start(s32[64]{0:T(128)S(1)} %fusion.104) | copy-start | bytes 772
  14.7 33.9 %all-to-all-start = ((s32[64,2,2]{1,2,0:T(2,128)}), s32[64,2,2]{1,2,0:T(2,128)S(1)}, u32[]{:S(2)}, u32[]{:S(2)}) async-start(s32[64,2,2]{1,2,0:T(2,128)} %copy.34), calls=%async_computation | async-start | bytes 131072 | tf_op jit(solution)/shard_map/all_to_all | solution.py:96
  35.6 23.1 %copy-start.3 = (bf16[1024,384]{1,0:T(8,128)(2,1)S(1)}, bf16[1024,384]{1,0:T(8,128)(2,1)}, u32[]{:S(2)}) copy-start(bf16[1024,384]{1,0:T(8,128)(2,1)} %param.19) | copy-start | bytes 2359300
  48.6 53.6 %all-to-all-start.1 = ((bf16[64,2,4,2,384]{4,2,3,1,0:T(4,128)(2,1)}), bf16[64,2,4,2,384]{4,2,3,1,0:T(4,128)(2,1)S(1)}, u32[]{:S(2)}, u32[]{:S(2)}) async-start(bf16[64,2,4,2,384]{4,2,3,1,0:T(4,128)(2,1)} %bitcast.11), calls=%async_computation.1 | async-start | bytes 1572864 | tf_op jit(solution)/shard_map/all_to_all | solution.py:95
  59.1 43.5 %copy-start.108 = (f32[384]{0:T(512)S(1)}, f32[384]{0:T(512)}, u32[]{:S(2)}) copy-start(f32[384]{0:T(512)} %param.12) | copy-start | bytes 4612
  59.7 42.5 %copy-start.6 = (f32[384]{0:T(512)}, f32[384]{0:T(512)S(1)}, u32[]{:S(2)}) copy-start(f32[384]{0:T(512)S(1)} %get-tuple-element.67) | copy-start | bytes 4612
  59.7 42.5 %copy-start.8 = (f32[384]{0:T(512)}, f32[384]{0:T(512)S(1)}, u32[]{:S(2)}) copy-start(f32[384]{0:T(512)S(1)} %get-tuple-element.68) | copy-start | bytes 4612
  59.7 42.5 %copy-start.10 = (f32[384]{0:T(512)}, f32[384]{0:T(512)S(1)}, u32[]{:S(2)}) copy-start(f32[384]{0:T(512)S(1)} %get-tuple-element.69) | copy-start | bytes 4612
  59.7 42.5 %copy-start.12 = (f32[384]{0:T(512)}, f32[384]{0:T(512)S(1)}, u32[]{:S(2)}) copy-start(f32[384]{0:T(512)S(1)} %get-tuple-element.70) | copy-start | bytes 4612
  59.8 42.5 %copy-start.14 = (f32[384]{0:T(512)}, f32[384]{0:T(512)S(1)}, u32[]{:S(2)}) copy-start(f32[384]{0:T(512)S(1)} %get-tuple-element.71) | copy-start | bytes 4612
  59.8 42.5 %copy-start.16 = (f32[384]{0:T(512)}, f32[384]{0:T(512)S(1)}, u32[]{:S(2)}) copy-start(f32[384]{0:T(512)S(1)} %get-tuple-element.72) | copy-start | bytes 4612
  59.8 42.5 %copy-start.18 = (f32[384]{0:T(512)}, f32[384]{0:T(512)S(1)}, u32[]{:S(2)}) copy-start(f32[384]{0:T(512)S(1)} %get-tuple-element.73) | copy-start | bytes 4612
  59.8 42.5 %copy-start.20 = (f32[384]{0:T(512)}, f32[384]{0:T(512)S(1)}, u32[]{:S(2)}) copy-start(f32[384]{0:T(512)S(1)} %get-tuple-element.74) | copy-start | bytes 4612
  59.8 42.5 %copy-start.22 = (f32[384]{0:T(512)}, f32[384]{0:T(512)S(1)}, u32[]{:S(2)}) copy-start(f32[384]{0:T(512)S(1)} %get-tuple-element.75) | copy-start | bytes 4612
  59.8 42.5 %copy-start.24 = (f32[384]{0:T(512)}, f32[384]{0:T(512)S(1)}, u32[]{:S(2)}) copy-start(f32[384]{0:T(512)S(1)} %get-tuple-element.76) | copy-start | bytes 4612
  59.8 42.5 %copy-start.26 = (f32[384]{0:T(512)}, f32[384]{0:T(512)S(1)}, u32[]{:S(2)}) copy-start(f32[384]{0:T(512)S(1)} %get-tuple-element.77) | copy-start | bytes 4612
  59.8 42.5 %copy-start.28 = (f32[384]{0:T(512)}, f32[384]{0:T(512)S(1)}, u32[]{:S(2)}) copy-start(f32[384]{0:T(512)S(1)} %get-tuple-element.78) | copy-start | bytes 4612
  59.8 42.5 %copy-start.30 = (f32[384]{0:T(512)}, f32[384]{0:T(512)S(1)}, u32[]{:S(2)}) copy-start(f32[384]{0:T(512)S(1)} %get-tuple-element.79) | copy-start | bytes 4612
  59.8 42.5 %copy-start.32 = (f32[384]{0:T(512)}, f32[384]{0:T(512)S(1)}, u32[]{:S(2)}) copy-start(f32[384]{0:T(512)S(1)} %get-tuple-element.80) | copy-start | bytes 4612
  59.9 42.5 %copy-start.34 = (f32[384]{0:T(512)}, f32[384]{0:T(512)S(1)}, u32[]{:S(2)}) copy-start(f32[384]{0:T(512)S(1)} %get-tuple-element.81) | copy-start | bytes 4612
  59.9 42.5 %copy-start.36 = (f32[384]{0:T(512)}, f32[384]{0:T(512)S(1)}, u32[]{:S(2)}) copy-start(f32[384]{0:T(512)S(1)} %get-tuple-element.82) | copy-start | bytes 4612
  59.9 42.5 %copy-start.38 = (f32[384]{0:T(512)}, f32[384]{0:T(512)S(1)}, u32[]{:S(2)}) copy-start(f32[384]{0:T(512)S(1)} %get-tuple-element.83) | copy-start | bytes 4612
  59.9 42.5 %copy-start.40 = (f32[384]{0:T(512)}, f32[384]{0:T(512)S(1)}, u32[]{:S(2)}) copy-start(f32[384]{0:T(512)S(1)} %get-tuple-element.84) | copy-start | bytes 4612
  60.0 42.4 %copy-start.42 = (f32[384]{0:T(512)}, f32[384]{0:T(512)S(1)}, u32[]{:S(2)}) copy-start(f32[384]{0:T(512)S(1)} %get-tuple-element.48) | copy-start | bytes 4612
  60.0 42.4 %copy-start.44 = (f32[384]{0:T(512)}, f32[384]{0:T(512)S(1)}, u32[]{:S(2)}) copy-start(f32[384]{0:T(512)S(1)} %get-tuple-element.49) | copy-start | bytes 4612
  60.0 42.4 %copy-start.46 = (f32[384]{0:T(512)}, f32[384]{0:T(512)S(1)}, u32[]{:S(2)}) copy-start(f32[384]{0:T(512)S(1)} %get-tuple-element.50) | copy-start | bytes 4612
  60.0 42.4 %copy-start.48 = (f32[384]{0:T(512)}, f32[384]{0:T(512)S(1)}, u32[]{:S(2)}) copy-start(f32[384]{0:T(512)S(1)} %get-tuple-element.51) | copy-start | bytes 4612
  60.0 42.4 %copy-start.50 = (f32[384]{0:T(512)}, f32[384]{0:T(512)S(1)}, u32[]{:S(2)}) copy-start(f32[384]{0:T(512)S(1)} %get-tuple-element.52) | copy-start | bytes 4612
  60.0 42.4 %copy-start.52 = (f32[384]{0:T(512)}, f32[384]{0:T(512)S(1)}, u32[]{:S(2)}) copy-start(f32[384]{0:T(512)S(1)} %get-tuple-element.53) | copy-start | bytes 4612
  60.1 42.4 %copy-start.54 = (f32[384]{0:T(512)}, f32[384]{0:T(512)S(1)}, u32[]{:S(2)}) copy-start(f32[384]{0:T(512)S(1)} %get-tuple-element.54) | copy-start | bytes 4612
  60.1 42.4 %copy-start.56 = (f32[384]{0:T(512)}, f32[384]{0:T(512)S(1)}, u32[]{:S(2)}) copy-start(f32[384]{0:T(512)S(1)} %get-tuple-element.55) | copy-start | bytes 4612
  60.1 42.4 %copy-start.58 = (f32[384]{0:T(512)}, f32[384]{0:T(512)S(1)}, u32[]{:S(2)}) copy-start(f32[384]{0:T(512)S(1)} %get-tuple-element.56) | copy-start | bytes 4612
  60.1 42.4 %copy-start.60 = (f32[384]{0:T(512)}, f32[384]{0:T(512)S(1)}, u32[]{:S(2)}) copy-start(f32[384]{0:T(512)S(1)} %get-tuple-element.57) | copy-start | bytes 4612
  60.1 42.4 %copy-start.62 = (f32[384]{0:T(512)}, f32[384]{0:T(512)S(1)}, u32[]{:S(2)}) copy-start(f32[384]{0:T(512)S(1)} %get-tuple-element.58) | copy-start | bytes 4612
  60.1 42.4 %copy-start.64 = (f32[384]{0:T(512)}, f32[384]{0:T(512)S(1)}, u32[]{:S(2)}) copy-start(f32[384]{0:T(512)S(1)} %get-tuple-element.59) | copy-start | bytes 4612
  60.1 42.4 %copy-start.66 = (f32[384]{0:T(512)}, f32[384]{0:T(512)S(1)}, u32[]{:S(2)}) copy-start(f32[384]{0:T(512)S(1)} %get-tuple-element.60) | copy-start | bytes 4612
  60.1 42.4 %copy-start.68 = (f32[384]{0:T(512)}, f32[384]{0:T(512)S(1)}, u32[]{:S(2)}) copy-start(f32[384]{0:T(512)S(1)} %get-tuple-element.61) | copy-start | bytes 4612
  60.1 42.4 %copy-start.70 = (f32[384]{0:T(512)}, f32[384]{0:T(512)S(1)}, u32[]{:S(2)}) copy-start(f32[384]{0:T(512)S(1)} %get-tuple-element.62) | copy-start | bytes 4612
  60.1 42.4 %copy-start.72 = (f32[384]{0:T(512)}, f32[384]{0:T(512)S(1)}, u32[]{:S(2)}) copy-start(f32[384]{0:T(512)S(1)} %get-tuple-element.63) | copy-start | bytes 4612
  60.2 42.4 %copy-start.74 = (f32[384]{0:T(512)}, f32[384]{0:T(512)S(1)}, u32[]{:S(2)}) copy-start(f32[384]{0:T(512)S(1)} %get-tuple-element.64) | copy-start | bytes 4612
  60.2 42.4 %copy-start.76 = (f32[384]{0:T(512)}, f32[384]{0:T(512)S(1)}, u32[]{:S(2)}) copy-start(f32[384]{0:T(512)S(1)} %get-tuple-element.65) | copy-start | bytes 4612
  60.9 41.7 %copy-start.78 = (f32[384]{0:T(512)}, f32[384]{0:T(512)S(1)}, u32[]{:S(2)}) copy-start(f32[384]{0:T(512)S(1)} %get-tuple-element.85) | copy-start | bytes 4612
  60.9 41.7 %copy-start.80 = (f32[384]{0:T(512)}, f32[384]{0:T(512)S(1)}, u32[]{:S(2)}) copy-start(f32[384]{0:T(512)S(1)} %get-tuple-element.86) | copy-start | bytes 4612
  60.9 41.7 %copy-start.82 = (f32[384]{0:T(512)}, f32[384]{0:T(512)S(1)}, u32[]{:S(2)}) copy-start(f32[384]{0:T(512)S(1)} %get-tuple-element.87) | copy-start | bytes 4612
  173.5 12.1 %copy-start.7 = (f32[384]{0:T(512)S(1)}, f32[384]{0:T(512)}, u32[]{:S(2)}) copy-start(f32[384]{0:T(512)} %copy-done.6) | copy-start | bytes 4612
  185.6 13.4 %copy-start = (f32[128,4,2,384]{3,1,2,0:T(4,128)}, f32[128,4,2,384]{3,1,2,0:T(4,128)S(1)}, u32[]{:S(2)}) copy-start(f32[128,4,2,384]{3,1,2,0:T(4,128)S(1)} %get-tuple-element.100) | copy-start | bytes 4718596
  199.0 52.2 %all-to-all-start.2 = ((bf16[64,2,4,2,384]{4,2,3,1,0:T(4,128)(2,1)}), bf16[64,2,4,2,384]{4,2,3,1,0:T(4,128)(2,1)}, u32[]{:S(2)}, u32[]{:S(2)}) async-start(bf16[64,2,4,2,384]{4,2,3,1,0:T(4,128)(2,1)} %bitcast.29), calls=%async_computation.2 | async-start | bytes 1572864 | tf_op jit(solution)/shard_map/all_to_all | solution.py:108
  206.2 272.2 %all-reduce.6.cloned.1.call-start = ((), (), s32[]{:S(2)}) async-start(), calls=%async_computation.3 | async-start | bytes 172032 | tf_op jit(solution)/shard_map/psum | solution.py:110
  (66 other events, 562.4 us)
Sparse Core Ops, SparseCore 0:
  214.5 263.9 all-reduce.5
where the time goes:
time: 488 us; the launch traced here: 487 us
  waiting for transfers between devices  297 us (61%)
  other arithmetic  56.3 us (12%)
  blocking collectives  48.6 us (10%)
  starting transfers between devices  36.1 us (7%)
  local copies, waits for them, and re-layouts  32.5 us (7%)
  between operations  16 us (3%)
    psum x1, waiting for transfers between devices, per_device(): param_grads = lax.psum(grads, 'dp')  224 us
    all_to_all x1, waiting for transfers between devices, per_device(): lax.all_to_all(send_tiles, 'dp', split_axis=0, concat_axis=0, tiled=True)  38.3 us
    all_to_all x1, waiting for transfers between devices, per_device(): lax.all_to_all(outgoing, 'dp', split_axis=0, concat_axis=0, tiled=True)  30 us
    psum x1, blocking collectives, backward_block(): lax.psum((jnp.sum(dnormed, -1), jnp.sum(dnormed * normed, -1)), 'enc')  26 us
    psum x1, blocking collectives, forward_block(): lax.psum((jnp.sum(filtered, -1), jnp.sum(filtered * filtered, -1)), 'enc')  22.6 us
    all_to_all x1, starting transfers between devices, per_device(): lax.all_to_all(send_meta, 'dp', split_axis=0, concat_axis=0, tiled=True)  18.7 us
    convert_element_type x1, other arithmetic, per_device(): outgoing = dtiles.astype(jnp.bfloat16).reshape(peers, cap, hgt, wid, chans)  13.1 us
    add x1, other arithmetic, forward_block(): filtered = conv_apply(tiles, kernel) + bias  11.8 us
  transfers between devices with their start and end apart: 4, of which 4 were waited for; matrix products, arithmetic and copies ran while one was open for 7% of the time, Pallas kernels for 0%

commit v1 on v0

v1 whole, which is shorter than its diff:
```python
import functools

import jax
import jax.numpy as jnp
from jax import lax
from jax.experimental import pallas as pl
from jax.experimental.pallas import tpu as pltpu
from jax.sharding import Mesh
from jax.sharding import PartitionSpec as P

EPS = 1e-06
HGT, WID = 4, 2
POS = HGT * WID
LANES = 128
DP = ("zh", "zl", "y")
ENC = ("x", "core")
VMEM_LIMIT = 16 * 1024 * 1024


def full(a, b):
    (ha, wa), (hb, wb) = divmod(a, WID), divmod(b, WID)
    return (hb - ha + 3) * 7 + (wb - wa + 3)


USED = sorted({full(a, b) for a in range(POS) for b in range(POS)})
PLACE = {tap: i for i, tap in enumerate(USED)}
ROWS = len(USED) + 3


def pack_kernel(peers, cap, part, ints_hbm, tiles_ref, send_ref, slot_ref, rows, data, seen, ints, sem):
    fetch = pltpu.make_async_copy(ints_hbm, ints, sem)
    fetch.start()
    tiles = tiles_ref.shape[0] // POS
    cbs = tiles_ref.shape[1] // LANES
    meta = cbs * cap * POS
    data[...] = jnp.zeros_like(data)
    for cb in range(cbs):
        rows[cb] = tiles_ref[:, cb * LANES : (cb + 1) * LANES].astype(jnp.float32)

    def clear(i, c):
        seen[i] = 0
        return c

    lax.fori_loop(0, peers, clear, 0, unroll=8)
    fetch.wait()
    lane = lax.broadcasted_iota(jnp.int32, (1, LANES), 1)

    def move(t, carry):
        s, end = carry
        step = (t >= end).astype(jnp.int32)
        s = s + step
        count = ints[0, 2 * tiles + s]
        end = end + step * count
        d = ints[0, t]
        r = seen[d]
        seen[d] = r + 1
        slot_ref[t] = d * cap + r
        for cb in range(cbs):
            at = d * part + cb * cap * POS + r * POS
            data[pl.ds(at, POS), :] = rows[cb, pl.ds(pl.multiple_of(t * POS, POS), POS), :]
        note = jnp.where(lane == r, ints[0, tiles + t], jnp.where(lane == cap + r, count, 0))
        here = pl.ds(d * part + meta, 1)
        data[here, :] = data[here, :] + note.astype(jnp.float32)
        return s, end

    lax.fori_loop(0, tiles, move, (jnp.int32(0), ints[0, 2 * tiles]), unroll=4)
    send_ref[...] = data[...].astype(jnp.bfloat16)


def conv_kernel(peers, cap, part, got_ref, seq_ref, kern_ref, bias_ref, gain_ref, scale_ref,
                x_ref, u_ref, f_ref, sums_ref, off_ref,
                data, seq, ups, cols, off_v, wgt_v, off_s, wgt_s, sem):
    cbs = seq_ref.shape[1] // LANES
    slots = peers * cap
    blocks = seq_ref.shape[0] // POS
    meta = cbs * cap * POS
    data[...] = got_ref[...].astype(jnp.float32)
    notes = data[pl.ds(meta, peers, stride=part), :]
    notes = jnp.concatenate([notes, jnp.zeros((LANES - peers, LANES), jnp.float32)], 0).T
    count = notes[cap : 2 * cap]
    off_v[0:cap] = jnp.where(count > 0.5, notes[0:cap], float(blocks)).astype(jnp.int32)
    wgt_v[0:cap] = jnp.where(count > 0.5, 8.0 / jnp.maximum(count, 1.0), 0.0)
    moves = [pltpu.make_async_copy(off_v, off_s, sem.at[0]), pltpu.make_async_copy(wgt_v, wgt_s, sem.at[1])]
    for m in moves:
        m.start()
    for cb in range(cbs):
        seq[cb, 0 : blocks * POS, :] = seq_ref[:, cb * LANES : (cb + 1) * LANES].astype(jnp.float32)
        seq[cb, blocks * POS :, :] = jnp.zeros((POS, LANES), jnp.float32)
    for m in moves:
        m.wait()
    for r in range(cap):

        def fetch(d, c, r=r):
            off, w = off_s[r, d], wgt_s[r, d]
            off_ref[r * peers + d] = off
            for cb in range(cbs):
                ups[cb, pl.ds(pl.multiple_of((r * peers + d) * POS, POS), POS), :] = (
                    seq[cb, pl.ds(pl.multiple_of(off * POS, POS), POS), :] * w
                )
            return c

        lax.fori_loop(0, peers, fetch, 0, unroll=8)
    lane = lax.broadcasted_iota(jnp.int32, (8, LANES), 1)
    for r in range(cap):

        def body(b, c, r=r):
            here = pl.ds(pl.multiple_of(r * peers + b * 8, 8), 8)
            xs = {}
            for cb in range(cbs):
                for q in range(POS):
                    x = data[pl.ds(b * 8 * part + cb * cap * POS + r * POS + q, 8, stride=part), :]
                    x_ref[cb, q, here, :] = x
                    xs[cb, q] = x
            out = jnp.zeros((8, LANES), jnp.float32)
            for p in range(POS):
                tot = [None] * 4
                for cb in range(cbs):
                    ch = slice(cb * LANES, (cb + 1) * LANES)
                    f = bias_ref[:, ch] + kern_ref[full(p, 0) : full(p, 0) + 1, ch] * xs[cb, 0]
                    for q in range(1, POS):
                        f = f + kern_ref[full(p, q) : full(p, q) + 1, ch] * xs[cb, q]
                    f_ref[cb, p, here, :] = f
                    u = ups[cb, pl.ds((r * peers + b * 8) * POS + p, 8, stride=POS), :]
                    u_ref[cb, p, here, :] = u
                    dn = u * (scale_ref[:, ch] * gain_ref[:, ch])
                    new = [f, f * f, dn, dn * f]
                    tot = new if cb == 0 else [a + n for a, n in zip(tot, new)]
                for k in range(4):
                    out = jnp.where(lane == k * POS + p, jnp.sum(tot[k], 1, keepdims=True), out)
            cols[here, :] = out
            return c

        lax.fori_loop(0, peers // 8, body, 0)
    total = cols[...].T[0 : 4 * POS]
    for i in range(sums_ref.shape[0]):
        sums_ref[i] = total


def stats_columns(sums_ref, width):
    sums = sums_ref[0]
    for i in range(1, sums_ref.shape[0]):
        sums = sums + sums_ref[i]
    center = sums[0:POS] / width
    inv = lax.rsqrt(jnp.maximum(sums[POS : 2 * POS] / width - center * center, 0.0) + EPS)
    first = sums[2 * POS : 3 * POS]
    second = inv * (sums[3 * POS : 4 * POS] - center * first)
    slots = sums.shape[1]
    rows = [center, inv, first / width, second / width, jnp.zeros((LANES - 4 * POS, slots), jnp.float32)]
    return jnp.concatenate(rows, 0).T


def grad_kernel(peers, cap, width, sums_ref, x_ref, u_ref, f_ref, kern_ref, gain_ref, scale_ref,
                out_ref, part_ref, stats, data, acc):
    cbs = x_ref.shape[0]
    part = cbs * cap * POS
    stats[...] = stats_columns(sums_ref, width)
    acc[...] = jnp.zeros_like(acc)
    for cb in range(cbs):
        ch = slice(cb * LANES, (cb + 1) * LANES)
        for r in range(cap):

            def body(b, c, r=r, cb=cb, ch=ch):
                here = pl.ds(pl.multiple_of(r * peers + b * 8, 8), 8)
                st = stats[here, :]

                def add(row, v):
                    acc[row, :, ch] = acc[row, :, ch] + v

                df, xs, us = [], [], []
                a_sum = b_sum = d_sum = None
                for p in range(POS):
                    col = [st[:, k * POS + p : k * POS + p + 1] for k in range(4)]
                    u = u_ref[cb, p, here, :]
                    n = (f_ref[cb, p, here, :] - col[0]) * col[1]
                    d = col[1] * (u * (scale_ref[:, ch] * gain_ref[:, ch]) - col[2] - n * col[3])
                    df.append(d)
                    us.append(u)
                    xs.append(x_ref[cb, p, here, :])
                    a_sum = u * n if p == 0 else a_sum + u * n
                    b_sum = u if p == 0 else b_sum + u
                    d_sum = d if p == 0 else d_sum + d
                taps = {}
                for p in range(POS):
                    for q in range(POS):
                        t = PLACE[full(p, q)]
                        v = df[p] * xs[q]
                        taps[t] = v if t not in taps else taps[t] + v
                for t, v in taps.items():
                    add(t, v)
                add(len(USED), d_sum)
                add(len(USED) + 1, a_sum)
                add(len(USED) + 2, b_sum)
                for q in range(POS):
                    t = us[q]
                    for p in range(POS):
                        t = t + kern_ref[full(p, q) : full(p, q) + 1, ch] * df[p]
                    data[pl.ds(b * 8 * part + cb * cap * POS + r * POS + q, 8, stride=part), :] = t
                return c

            lax.fori_loop(0, peers // 8, body, 0)
    out_ref[...] = data[...].astype(jnp.bfloat16)
    for row in range(ROWS):
        part_ref[row : row + 1, :] = jnp.sum(acc[row], 0, keepdims=True)


def token_kernel(peers, cap, width, off_ref, sums_ref, x_ref, f_ref, gain_ref, shift_ref, scale_ref,
                 vis_ref, stats, toks, data):
    cbs = x_ref.shape[0]
    slots = peers * cap
    stats[...] = stats_columns(sums_ref, width)
    data[...] = jnp.zeros_like(data)
    for cb in range(cbs):
        ch = slice(cb * LANES, (cb + 1) * LANES)

        def body(b, c, cb=cb, ch=ch):
            here = pl.ds(pl.multiple_of(b * 8, 8), 8)
            st = stats[here, :]
            for p in range(POS):
                n = (f_ref[cb, p, here, :] - st[:, p : p + 1]) * st[:, POS + p : POS + p + 1]
                m = n * gain_ref[:, ch] + shift_ref[:, ch]
                toks[cb, pl.ds(b * 8 * POS + p, 8, stride=POS), :] = x_ref[cb, p, here, :] + scale_ref[:, ch] * m
            return c

        lax.fori_loop(0, slots // 8, body, 0)

    def put(s, c):
        at = pl.ds(pl.multiple_of(off_ref[s] * POS, POS), POS)
        for cb in range(cbs):
            data[cb, at, :] = toks[cb, pl.ds(pl.multiple_of(s * POS, POS), POS), :]
        return c

    lax.fori_loop(0, slots, put, 0, unroll=8)
    for cb in range(cbs):
        vis_ref[:, cb * LANES : (cb + 1) * LANES] = data[cb, 0 : vis_ref.shape[0], :].astype(jnp.bfloat16)


def unpack_kernel(cap, slot_ref, back_ref, out_ref, data, rows):
    tiles = slot_ref.shape[0]
    cbs = out_ref.shape[1] // LANES
    part = cbs * cap * POS
    data[...] = back_ref[...].astype(jnp.float32)

    def move(t, c):
        slot = slot_ref[t]
        d, r = slot // cap, lax.rem(slot, cap)
        for cb in range(cbs):
            at = pl.multiple_of(d * part + cb * cap * POS + r * POS, POS)
            rows[cb, pl.ds(pl.multiple_of(t * POS, POS), POS), :] = data[pl.ds(at, POS), :]
        return c

    lax.fori_loop(0, tiles, move, 0, unroll=8)
    for cb in range(cbs):
        out_ref[:, cb * LANES : (cb + 1) * LANES] = rows[cb].astype(jnp.bfloat16)


def finish_kernel(parts_ref, gain_ref, shift_ref, scale_ref, out_ref):
    total = parts_ref[0]
    for i in range(1, parts_ref.shape[0]):
        total = total + parts_ref[i]
    out_ref[...] = jnp.zeros_like(out_ref)
    n, taps = len(USED), out_ref.shape[0] - 4
    for i, tap in enumerate(USED):
        out_ref[tap : tap + 1, :] = total[i : i + 1]
    along, plain = total[n + 1 : n + 2], total[n + 2 : n + 3]
    out_ref[taps : taps + 1, :] = total[n : n + 1]
    out_ref[taps + 1 : taps + 2, :] = along * scale_ref[...]
    out_ref[taps + 2 : taps + 3, :] = plain * scale_ref[...]
    out_ref[taps + 3 : taps + 4, :] = along * gain_ref[...] + plain * shift_ref[...]


ANY = pl.BlockSpec(memory_space=pl.ANY)
SMEM = pl.BlockSpec(memory_space=pltpu.SMEM)
VMEM = pl.BlockSpec(memory_space=pltpu.VMEM)


def call(kernel, ins, outs, scratch, out_specs):
    return pl.pallas_call(
        kernel,
        out_shape=outs,
        in_specs=ins,
        out_specs=out_specs,
        scratch_shapes=scratch,
        compiler_params=pltpu.CompilerParams(vmem_limit_bytes=VMEM_LIMIT),
    )


def per_device(tile_features, dw_kernel, dw_bias, ln_gain, ln_shift, layer_scale,
               sample_counts, tile_dest, tile_offset, seq_grad):
    tiles_dev, _, _, chans = tile_features.shape
    enc = lax.axis_size(ENC)
    width = float(chans * enc)
    peers = lax.axis_size(DP)
    cap = tiles_dev // peers + 1
    slots, cbs = peers * cap, chans // LANES
    blocks = seq_grad.shape[0] // POS
    part_out = cbs * cap * POS
    part = part_out + 2
    f32, i32, bf16 = jnp.float32, jnp.int32, jnp.bfloat16
    shape = jax.ShapeDtypeStruct
    bias, gain, shift, scale = (v.reshape(1, chans) for v in (dw_bias, ln_gain, ln_shift, layer_scale))
    grid = shape((cbs, POS, slots, LANES), f32)

    ints = jnp.concatenate([tile_dest, tile_offset, sample_counts], 1)
    send, slot = call(
        functools.partial(pack_kernel, peers, cap, part),
        [ANY, VMEM],
        (shape((peers * part, LANES), bf16), shape((tiles_dev,), i32)),
        [pltpu.VMEM((cbs, tiles_dev * POS, LANES), f32), pltpu.VMEM((peers * part, LANES), f32), pltpu.SMEM((peers,), i32),
         pltpu.SMEM(ints.shape, i32), pltpu.SemaphoreType.DMA],
        (VMEM, SMEM),
    )(ints, tile_features.reshape(tiles_dev * POS, chans))
    got = lax.all_to_all(send.reshape(peers, part // 2, 2, LANES), DP, split_axis=0, concat_axis=0, tiled=True)
    x, u, f, sums, off = call(
        functools.partial(conv_kernel, peers, cap, part),
        [VMEM] * 6,
        (grid, grid, grid, shape((enc, 4 * POS, slots), f32), shape((slots,), i32)),
        [
            pltpu.VMEM((peers * part, LANES), f32),
            pltpu.VMEM((cbs, (blocks + 1) * POS, LANES), f32),
            pltpu.VMEM((cbs, slots * POS, LANES), f32),
            pltpu.VMEM((slots, LANES), f32),
            pltpu.VMEM((8, LANES), i32),
            pltpu.VMEM((8, LANES), f32),
            pltpu.SMEM((8, LANES), i32),
            pltpu.SMEM((8, LANES), f32),
            pltpu.SemaphoreType.DMA((2,)),
        ],
        (VMEM, VMEM, VMEM, VMEM, SMEM),
    )(got.reshape(peers * part, LANES), seq_grad, dw_kernel, bias, gain, scale)
    sums = lax.all_to_all(sums, ENC, split_axis=0, concat_axis=0, tiled=True)
    outgoing, grads = call(
        functools.partial(grad_kernel, peers, cap, width),
        [VMEM] * 7,
        (shape((peers * part_out, LANES), bf16), shape((ROWS, chans), f32)),
        [pltpu.VMEM((slots, LANES), f32), pltpu.VMEM((peers * part_out, LANES), f32), pltpu.VMEM((ROWS, 8, chans), f32)],
        (VMEM, VMEM),
    )(sums, x, u, f, dw_kernel, gain, scale)
    back = lax.all_to_all(outgoing.reshape(peers, part_out, LANES), DP, split_axis=0, concat_axis=0, tiled=True)
    grads = lax.psum(lax.psum(grads, "y"), "zh")
    inner = lax.axis_size("zl")
    grads, back, off, sums = lax.optimization_barrier((grads, back, off, sums))
    parts = lax.all_to_all(
        jnp.broadcast_to(grads, (inner, ROWS, chans)), "zl", split_axis=0, concat_axis=0, tiled=True
    )
    tile_grads = call(
        functools.partial(unpack_kernel, cap),
        [SMEM, VMEM],
        shape((tiles_dev * POS, chans), bf16),
        [pltpu.VMEM((peers * part_out, LANES), f32), pltpu.VMEM((cbs, tiles_dev * POS, LANES), f32)],
        VMEM,
    )(slot, back.reshape(peers * part_out, LANES))
    vis = call(
        functools.partial(token_kernel, peers, cap, width),
        [SMEM] + [VMEM] * 6,
        shape((blocks * POS, chans), bf16),
        [
            pltpu.VMEM((slots, LANES), f32),
            pltpu.VMEM((cbs, slots * POS, LANES), f32),
            pltpu.VMEM((cbs, (blocks + 1) * POS, LANES), f32),
        ],
        VMEM,
    )(off, sums, x, f, gain, shift, scale)
    param_grads = call(
        finish_kernel, [VMEM] * 4, shape((dw_kernel.shape[0] + 4, chans), f32), [], VMEM
    )(parts, gain, shift, scale)
    return vis, tile_grads.reshape(tile_features.shape), param_grads


def solution(mesh):
    grid = Mesh(mesh.devices.reshape(4, 4, 4, 4, 2), DP + ENC)
    placed = (
        P(DP, None, None, ENC),
        P(None, ENC),
        P(ENC),
        P(ENC),
        P(ENC),
        P(ENC),
        P(DP, None),
        P(DP, None),
        P(DP, None),
        P(DP, ENC),
    )
    return jax.shard_map(
        per_device,
        mesh=grid,
        in_specs=placed,
        out_specs=(P(DP, ENC), P(DP, None, None, ENC), P(None, ENC)),
        check_vma=False,
    )
```

time: 488 us -> 175 us (0.36)
  the two profiles are of different devices: /device:TPU:4 before, /device:TPU:40 now
where the time goes in v1:
time: 175 us
  blocking collectives  65.4 us (37%)
  waiting for transfers between devices  44.1 us (25%)
  starting transfers between devices  31.3 us (18%)
  Pallas kernels  23.8 us (14%)
  local copies, waits for them, and re-layouts  8.39 us (5%)
    psum x2, blocking collectives, per_device(): grads = lax.psum(lax.psum(grads, 'y'), 'zh')  55.2 us
    all_to_all x1, waiting for transfers between devices, per_device(): lax.all_to_all(send.reshape(peers, part // 2, 2, LANES), DP, split_axis=0...  44.1 us
    all_to_all x1, starting transfers between devices, per_device(): lax.all_to_all(send.reshape(peers, part // 2, 2, LANES), DP, split_axis=0...  18.3 us
    all_to_all x1, blocking collectives, per_device(): sums = lax.all_to_all(sums, ENC, split_axis=0, concat_axis=0, tiled=True)  10.2 us
    all_to_all x1, starting transfers between devices, per_device(): lax.all_to_all(outgoing.reshape(peers, part_out, LANES), DP, split_axis=0...  7.4 us
    pallas_call x1, Pallas kernels, per_device(): call(functools.partial(grad_kernel, peers, cap, width), [VMEM] * 7, (shap...  7.02 us
    pallas_call x1, Pallas kernels, per_device(): call(functools.partial(token_kernel, peers, cap, width), [SMEM] + [VMEM]...  6.63 us
    unnamed x26, local copies, waits for them, and re-layouts  5.64 us
  transfers between devices with their start and end apart: 3, of which 1 were waited for; matrix products, arithmetic and copies ran while one was open for 1% of the time, Pallas kernels for 5%

profile of v1, /device:TPU:40, one launch (start us, length us, event | category | flops | bytes accessed | tf_op | source)
XLA Modules:
  0.0 174.7 jit_solution(10047112978317871742)
XLA Ops:
  0.6 0.0 copy-start.9
  0.6 0.0 copy-start.10
  0.7 0.0 copy-start.11
  0.7 0.0 copy-start.6
  0.7 1.2 reshape.36.tiles_ref
  1.9 0.8 pad_add_fusion.ints_hbm
  2.6 2.1 %shard_map.121 = (bf16[3200,128]{1,0:T(8,128)(2,1)}, s32[64]{0:T(128)S(1)}) custom-call(s32[1,136]{1,0:T(1,128)S(1)} %pad_add_fusion.ints_hbm, bf16[512,384]{1,0:T(8,128)(2,1)S(1)} %reshape.36.tiles_ref), custom_call_target="tpu_custom_call" | custom-call | tf_op jit(solution)/shard_map/pallas_call | solution.py:304
  4.7 18.3 %all-to-all-start = ((bf16[64,25,2,128]{3,2,1,0:T(2,128)(2,1)}), bf16[64,25,2,128]{3,2,1,0:T(2,128)(2,1)S(1)}, u32[]{:S(2)}, u32[]{:S(2)}) async-start(bf16[64,25,2,128]{3,2,1,0:T(2,128)(2,1)} %bitcast), calls=%async_computation | async-start | bytes 1638400 | tf_op jit(solution)/shard_map/all_to_all | solution.py:312
  23.0 0.0 copy-done.9
  23.1 0.0 copy-done.10
  23.1 0.0 copy-done.11
  23.1 44.1 %all-to-all-done = bf16[64,25,2,128]{3,2,1,0:T(2,128)(2,1)S(1)} async-done(((bf16[64,25,2,128]{3,2,1,0:T(2,128)(2,1)}), bf16[64,25,2,128]{3,2,1,0:T(2,128)(2,1)S(1)}, u32[]{:S(2)}, u32[]{:S(2)}) %all-to-all-start) | async-done | bytes 819232 | tf_op jit(solution)/shard_map/all_to_all | solution.py:312
  67.2 0.0 copy-start
  67.2 0.9 copy-done
  68.1 0.0 copy-done.6
  68.1 0.0 copy-start.1
  68.1 1.1 copy-done.1
  69.3 0.0 copy-start.4
  69.3 1.1 copy-done.4
  70.4 4.8 %shard_map.122 = (f32[3,8,128,128]{3,2,1,0:T(8,128)S(1)}, f32[3,8,128,128]{3,2,1,0:T(8,128)S(1)}, f32[3,8,128,128]{3,2,1,0:T(8,128)S(1)}, f32[8,32,128]{2,1,0:T(8,128)S(1)}, s32[128]{0:T(128)S(1)}) custom-call(bf16[3200,128]{1,0:T(8,128)(2,1)S(1)} %bitcast.4, bf16[1024,384]{1,0:T(8,128)(2,1)S(1)} %copy-done.4, f32[49,384]{1,0:T(8,128)S(1)} %copy-done.6, ...), custom_call_target="tpu_custom_call" | custom-call | tf_op jit(solution)/shard_map/pallas_call | solution.py:313
  75.2 0.0 copy-start.7
  75.2 10.2 %all_to_all.20.sums_ref = f32[8,32,128]{2,1,0:T(8,128)S(1)} all-to-all(f32[8,32,128]{2,1,0:T(8,128)S(1)} %get-tuple-element.17), channel_id=1, replica_groups=mesh['zh'=4,'zl'=4,'y'=4,'x'=4,'core'=2] {'x','core'}, dimensions={0} | all-to-all | bytes 262144 | tf_op jit(solution)/shard_map/all_to_all | solution.py:330
  85.4 0.0 copy-start.2
  85.4 7.0 %shard_map.123 = (bf16[3072,128]{1,0:T(8,128)(2,1)S(1)}, f32[24,384]{1,0:T(8,128)S(1)}) custom-call(f32[8,32,128]{2,1,0:T(8,128)S(1)} %all_to_all.20.sums_ref, f32[3,8,128,128]{3,2,1,0:T(8,128)S(1)} %get-tuple-element.18.x_ref, f32[3,8,128,128]{3,2,1,0:T(8,128)S(1)} %get-tuple-element.19.u_ref, f32[3,8,128,128]{3,2,1,0:T(8,128)S(1)} %get-tuple-element.20.f_ref, ...), custom_call_target="tpu_custom_call" | custom-call | tf_op jit(solution)/shard_map/pallas_call | solution.py:331
  92.5 0.0 copy-done.7
  92.5 0.0 copy-done.2
  92.5 0.0 copy-start.5
  92.5 0.9 copy-done.5
  93.4 0.0 copy-start.12
  93.4 7.4 %all-to-all-start.2 = ((bf16[64,48,128]{2,1,0:T(8,128)(2,1)}), bf16[64,48,128]{2,1,0:T(8,128)(2,1)}, u32[]{:S(2)}, u32[]{:S(2)}) async-start(bf16[64,48,128]{2,1,0:T(8,128)(2,1)} %bitcast.5), calls=%async_computation.2 | async-start | bytes 1572864 | tf_op jit(solution)/shard_map/all_to_all | solution.py:338
  100.8 14.6 %psum.14 = f32[24,384]{1,0:T(8,128)S(1)} all-reduce(f32[24,384]{1,0:T(8,128)S(1)} %get-tuple-element.21), channel_id=1, replica_groups=mesh['zh'=4,'zl'=4,'y'=4,'x'=4,'core'=2] {'y'}, use_global_device_ids=true, to_apply=%region_0.0 | all-reduce | flops 9216 | bytes 73728 | tf_op jit(solution)/shard_map/psum | solution.py:339
  115.4 40.6 %psum.15 = f32[24,384]{1,0:T(8,128)S(1)} all-reduce(f32[24,384]{1,0:T(8,128)S(1)} %psum.14), channel_id=1, replica_groups=mesh['zh'=4,'zl'=4,'y'=4,'x'=4,'core'=2] {'zh'}, use_global_device_ids=true, to_apply=%region_1.0 | all-reduce | flops 9216 | bytes 73728 | tf_op jit(solution)/shard_map/psum | solution.py:339
  156.0 0.0 all-to-all-done.2
  156.0 0.7 broadcast_in_dim.3
  156.7 5.6 %all-to-all-start.3 = ((f32[4,24,384]{2,1,0:T(8,128)}), f32[4,24,384]{2,1,0:T(8,128)}, u32[]{:S(2)}, u32[]{:S(2)}) async-start(f32[4,24,384]{2,1,0:T(8,128)} %broadcast_in_dim.3), calls=%async_computation.3 | async-start | bytes 294912 | tf_op jit(solution)/shard_map/all_to_all | solution.py:342
  162.3 0.0 copy-done.12
  162.3 1.7 shard_map.125
  164.0 0.9 reshape.45
  164.9 0.0 copy-start.3
  164.9 0.9 copy-done.3
  165.8 0.0 copy-start.8
  165.8 0.7 copy-done.8
  166.5 6.6 %shard_map.124 = bf16[1024,384]{1,0:T(8,128)(2,1)} custom-call(s32[128]{0:T(128)S(1)} %copy-done.8, f32[8,32,128]{2,1,0:T(8,128)S(1)} %copy-done.3, f32[3,8,128,128]{3,2,1,0:T(8,128)S(1)} %get-tuple-element.18.x_ref, f32[3,8,128,128]{3,2,1,0:T(8,128)S(1)} %get-tuple-element.20.f_ref, f32[1,384]{1,0:T(1,128)S(1)} %reshape.40.gain_ref, ...), custom_call_target="tpu_custom_call" | custom-call | tf_op jit(solution)/shard_map/pallas_call | solution.py:352
  173.1 0.0 all-to-all-done.3.parts_ref
  173.1 1.6 shard_map.126
  (4 shorter events, 0.0 us)
Async XLA Ops:
  0.6 22.4 %copy-start.9 = (f32[384]{0:T(512)S(1)}, f32[384]{0:T(512)}, u32[]{:S(2)}) copy-start(f32[384]{0:T(512)} %param.13) | copy-start | bytes 4612
  0.6 22.4 %copy-start.10 = (f32[384]{0:T(512)S(1)}, f32[384]{0:T(512)}, u32[]{:S(2)}) copy-start(f32[384]{0:T(512)} %param.15) | copy-start | bytes 4612
  0.7 22.4 %copy-start.11 = (f32[384]{0:T(512)S(1)}, f32[384]{0:T(512)}, u32[]{:S(2)}) copy-start(f32[384]{0:T(512)} %param.12) | copy-start | bytes 4612
  0.7 67.5 %copy-start.6 = (f32[49,384]{1,0:T(8,128)S(1)}, f32[49,384]{1,0:T(8,128)}, u32[]{:S(2)}) copy-start(f32[49,384]{1,0:T(8,128)} %kern_ref.3) | copy-start | bytes 225796
  4.7 62.5 %all-to-all-start = ((bf16[64,25,2,128]{3,2,1,0:T(2,128)(2,1)}), bf16[64,25,2,128]{3,2,1,0:T(2,128)(2,1)S(1)}, u32[]{:S(2)}, u32[]{:S(2)}) async-start(bf16[64,25,2,128]{3,2,1,0:T(2,128)(2,1)} %bitcast), calls=%async_computation | async-start | bytes 1638400 | tf_op jit(solution)/shard_map/all_to_all | solution.py:312
  67.2 0.9 copy-start
  68.1 1.1 copy-start.1
  69.3 1.1 copy-start.4
  75.2 17.3 %copy-start.7 = (s32[128]{0:T(128)}, s32[128]{0:T(128)S(1)}, u32[]{:S(2)}) copy-start(s32[128]{0:T(128)S(1)} %get-tuple-element.24.off_ref) | copy-start | bytes 1540
  85.4 7.0 %copy-start.2 = (f32[8,32,128]{2,1,0:T(8,128)}, f32[8,32,128]{2,1,0:T(8,128)S(1)}, u32[]{:S(2)}) copy-start(f32[8,32,128]{2,1,0:T(8,128)S(1)} %all_to_all.20.sums_ref) | copy-start | bytes 393220
  92.5 0.9 copy-start.5
  93.4 68.9 %copy-start.12 = (f32[384]{0:T(512)S(1)}, f32[384]{0:T(512)}, u32[]{:S(2)}) copy-start(f32[384]{0:T(512)} %param.14) | copy-start | bytes 4612
  93.4 62.6 %all-to-all-start.2 = ((bf16[64,48,128]{2,1,0:T(8,128)(2,1)}), bf16[64,48,128]{2,1,0:T(8,128)(2,1)}, u32[]{:S(2)}, u32[]{:S(2)}) async-start(bf16[64,48,128]{2,1,0:T(8,128)(2,1)} %bitcast.5), calls=%async_computation.2 | async-start | bytes 1572864 | tf_op jit(solution)/shard_map/all_to_all | solution.py:338
  156.7 16.4 %all-to-all-start.3 = ((f32[4,24,384]{2,1,0:T(8,128)}), f32[4,24,384]{2,1,0:T(8,128)}, u32[]{:S(2)}, u32[]{:S(2)}) async-start(f32[4,24,384]{2,1,0:T(8,128)} %broadcast_in_dim.3), calls=%async_computation.3 | async-start | bytes 294912 | tf_op jit(solution)/shard_map/all_to_all | solution.py:342
  164.9 0.9 copy-start.3
  165.8 0.7 copy-start.8

commit v2 on v1

--- a/solution.py
+++ b/solution.py
@@ -68,11 +68,9 @@
 
 
 def conv_kernel(peers, cap, part, got_ref, seq_ref, kern_ref, bias_ref, gain_ref, scale_ref,
-                x_ref, u_ref, f_ref, sums_ref, off_ref,
-                data, seq, ups, cols, off_v, wgt_v, off_s, wgt_s, sem):
-    cbs = seq_ref.shape[1] // LANES
-    slots = peers * cap
-    blocks = seq_ref.shape[0] // POS
+                data, ups, f_ref, sums_ref, off_ref, seq, cols, off_v, wgt_v, off_s, wgt_s, sem):
+    cbs = seq.shape[0]
+    blocks = seq.shape[1] // POS - 1
     meta = cbs * cap * POS
     data[...] = got_ref[...].astype(jnp.float32)
     notes = data[pl.ds(meta, peers, stride=part), :]
@@ -108,9 +106,7 @@
             xs = {}
             for cb in range(cbs):
                 for q in range(POS):
-                    x = data[pl.ds(b * 8 * part + cb * cap * POS + r * POS + q, 8, stride=part), :]
-                    x_ref[cb, q, here, :] = x
-                    xs[cb, q] = x
+                    xs[cb, q] = data[pl.ds(b * 8 * part + cb * cap * POS + r * POS + q, 8, stride=part), :]
             out = jnp.zeros((8, LANES), jnp.float32)
             for p in range(POS):
                 tot = [None] * 4
@@ -121,7 +117,6 @@
                         f = f + kern_ref[full(p, q) : full(p, q) + 1, ch] * xs[cb, q]
                     f_ref[cb, p, here, :] = f
                     u = ups[cb, pl.ds((r * peers + b * 8) * POS + p, 8, stride=POS), :]
-                    u_ref[cb, p, here, :] = u
                     dn = u * (scale_ref[:, ch] * gain_ref[:, ch])
                     new = [f, f * f, dn, dn * f]
                     tot = new if cb == 0 else [a + n for a, n in zip(tot, new)]
@@ -149,19 +144,20 @@
     return jnp.concatenate(rows, 0).T
 
 
-def grad_kernel(peers, cap, width, sums_ref, x_ref, u_ref, f_ref, kern_ref, gain_ref, scale_ref,
-                out_ref, part_ref, stats, data, acc):
-    cbs = x_ref.shape[0]
-    part = cbs * cap * POS
+def grad_kernel(peers, cap, part, extra, width, sums_ref, data_ref, ups_ref, f_ref, kern_ref, gain_ref, scale_ref,
+                out_ref, stats, data, acc, even, odd):
+    cbs = f_ref.shape[0]
+    meta = cbs * cap * POS
+    back = meta + extra
     stats[...] = stats_columns(sums_ref, width)
     acc[...] = jnp.zeros_like(acc)
-    for cb in range(cbs):
-        ch = slice(cb * LANES, (cb + 1) * LANES)
-        for r in range(cap):
-
-            def body(b, c, r=r, cb=cb, ch=ch):
-                here = pl.ds(pl.multiple_of(r * peers + b * 8, 8), 8)
-                st = stats[here, :]
+    for r in range(cap):
+
+        def body(b, c, r=r):
+            here = pl.ds(pl.multiple_of(r * peers + b * 8, 8), 8)
+            st = stats[here, :]
+            for cb in range(cbs):
+                ch = slice(cb * LANES, (cb + 1) * LANES)
 
                 def add(row, v):
                     acc[row, :, ch] = acc[row, :, ch] + v
@@ -170,12 +166,12 @@
                 a_sum = b_sum = d_sum = None
                 for p in range(POS):
                     col = [st[:, k * POS + p : k * POS + p + 1] for k in range(4)]
-                    u = u_ref[cb, p, here, :]
+                    u = ups_ref[cb, pl.ds((r * peers + b * 8) * POS + p, 8, stride=POS), :]
                     n = (f_ref[cb, p, here, :] - col[0]) * col[1]
                     d = col[1] * (u * (scale_ref[:, ch] * gain_ref[:, ch]) - col[2] - n * col[3])
                     df.append(d)
                     us.append(u)
-                    xs.append(x_ref[cb, p, here, :])
+                    xs.append(data_ref[pl.ds(b * 8 * part + cb * cap * POS + r * POS + p, 8, stride=part), :])
                     a_sum = u * n if p == 0 else a_sum + u * n
                     b_sum = u if p == 0 else b_sum + u
                     d_sum = d if p == 0 else d_sum + d
@@ -194,34 +190,47 @@
                     t = us[q]
                     for p in range(POS):
                         t = t + kern_ref[full(p, q) : full(p, q) + 1, ch] * df[p]
-                    data[pl.ds(b * 8 * part + cb * cap * POS + r * POS + q, 8, stride=part), :] = t
-                return c
-
-            lax.fori_loop(0, peers // 8, body, 0)
+                    data[pl.ds(b * 8 * back + cb * cap * POS + r * POS + q, 8, stride=back), :] = t
+            return c
+
+        lax.fori_loop(0, peers // 8, body, 0)
+    for row in range(ROWS):
+        for cb in range(cbs):
+            v = row * cbs + cb
+            half = even if v % 2 == 0 else odd
+            half[v // 2 : v // 2 + 1, :] = jnp.sum(acc[row, :, cb * LANES : (cb + 1) * LANES], 0, keepdims=True)
+    holders = even.shape[0]
+    for i, half in enumerate((even, odd)):
+        sums = half[...]
+        high = sums.astype(jnp.bfloat16).astype(jnp.float32)
+        for j, v in ((i, high), (i + 2, sums - high)):
+            data[pl.ds(meta + j, holders, stride=back), :] = v
+    for j in range(extra):
+        data[pl.ds(holders * back + meta + j, peers - holders, stride=back), :] = jnp.zeros((peers - holders, LANES), jnp.float32)
     out_ref[...] = data[...].astype(jnp.bfloat16)
-    for row in range(ROWS):
-        part_ref[row : row + 1, :] = jnp.sum(acc[row], 0, keepdims=True)
-
-
-def token_kernel(peers, cap, width, off_ref, sums_ref, x_ref, f_ref, gain_ref, shift_ref, scale_ref,
+
+
+def token_kernel(peers, cap, part, width, off_ref, sums_ref, data_ref, f_ref, gain_ref, shift_ref, scale_ref,
                  vis_ref, stats, toks, data):
-    cbs = x_ref.shape[0]
+    cbs = f_ref.shape[0]
     slots = peers * cap
     stats[...] = stats_columns(sums_ref, width)
     data[...] = jnp.zeros_like(data)
-    for cb in range(cbs):
-        ch = slice(cb * LANES, (cb + 1) * LANES)
-
-        def body(b, c, cb=cb, ch=ch):
-            here = pl.ds(pl.multiple_of(b * 8, 8), 8)
+    for r in range(cap):
+
+        def body(b, c, r=r):
+            here = pl.ds(pl.multiple_of(r * peers + b * 8, 8), 8)
             st = stats[here, :]
-            for p in range(POS):
-                n = (f_ref[cb, p, here, :] - st[:, p : p + 1]) * st[:, POS + p : POS + p + 1]
-                m = n * gain_ref[:, ch] + shift_ref[:, ch]
-                toks[cb, pl.ds(b * 8 * POS + p, 8, stride=POS), :] = x_ref[cb, p, here, :] + scale_ref[:, ch] * m
+            for cb in range(cbs):
+                ch = slice(cb * LANES, (cb + 1) * LANES)
+                for p in range(POS):
+                    n = (f_ref[cb, p, here, :] - st[:, p : p + 1]) * st[:, POS + p : POS + p + 1]
+                    m = n * gain_ref[:, ch] + shift_ref[:, ch]
+                    x = data_ref[pl.ds(b * 8 * part + cb * cap * POS + r * POS + p, 8, stride=part), :]
+                    toks[cb, pl.ds((r * peers + b * 8) * POS + p, 8, stride=POS), :] = x + scale_ref[:, ch] * m
             return c
 
-        lax.fori_loop(0, slots // 8, body, 0)
+        lax.fori_loop(0, peers // 8, body, 0)
 
     def put(s, c):
         at = pl.ds(pl.multiple_of(off_ref[s] * POS, POS), POS)
@@ -234,17 +243,27 @@
         vis_ref[:, cb * LANES : (cb + 1) * LANES] = data[cb, 0 : vis_ref.shape[0], :].astype(jnp.bfloat16)
 
 
-def unpack_kernel(cap, slot_ref, back_ref, out_ref, data, rows):
+def total_kernel(meta, back, back_ref, out_ref):
+    peers = out_ref.shape[0]
+    rows = back_ref.shape[0]
+    at = lax.rem(lax.broadcasted_iota(jnp.int32, (8, rows), 1), back) - meta
+    which = lax.broadcasted_iota(jnp.int32, (8, rows), 0)
+    pick = jnp.where((at == which) | (at == which + 2), 1.0, 0.0)
+    pick = jnp.where(which < 2, pick, 0.0).astype(jnp.bfloat16)
+    total = jnp.dot(pick, back_ref[...], preferred_element_type=jnp.float32)[0:2]
+    out_ref[...] = jnp.broadcast_to(total[None], (peers, 2, LANES))
+
+
+def unpack_kernel(cap, part, slot_ref, back_ref, out_ref, data, rows):
     tiles = slot_ref.shape[0]
     cbs = out_ref.shape[1] // LANES
-    part = cbs * cap * POS
     data[...] = back_ref[...].astype(jnp.float32)
 
     def move(t, c):
         slot = slot_ref[t]
         d, r = slot // cap, lax.rem(slot, cap)
         for cb in range(cbs):
-            at = pl.multiple_of(d * part + cb * cap * POS + r * POS, POS)
+            at = d * part + cb * cap * POS + r * POS
             rows[cb, pl.ds(pl.multiple_of(t * POS, POS), POS), :] = data[pl.ds(at, POS), :]
         return c
 
@@ -254,18 +273,23 @@
 
 
 def finish_kernel(parts_ref, gain_ref, shift_ref, scale_ref, out_ref):
-    total = parts_ref[0]
-    for i in range(1, parts_ref.shape[0]):
-        total = total + parts_ref[i]
     out_ref[...] = jnp.zeros_like(out_ref)
     n, taps = len(USED), out_ref.shape[0] - 4
-    for i, tap in enumerate(USED):
-        out_ref[tap : tap + 1, :] = total[i : i + 1]
-    along, plain = total[n + 1 : n + 2], total[n + 2 : n + 3]
-    out_ref[taps : taps + 1, :] = total[n : n + 1]
-    out_ref[taps + 1 : taps + 2, :] = along * scale_ref[...]
-    out_ref[taps + 2 : taps + 3, :] = plain * scale_ref[...]
-    out_ref[taps + 3 : taps + 4, :] = along * gain_ref[...] + plain * shift_ref[...]
+    cbs = out_ref.shape[1] // LANES
+    for cb in range(cbs):
+        ch = slice(cb * LANES, (cb + 1) * LANES)
+
+        def total(i):
+            v = i * cbs + cb
+            return parts_ref[v // 2, v % 2 : v % 2 + 1, :]
+
+        for i, tap in enumerate(USED):
+            out_ref[tap : tap + 1, ch] = total(i)
+        along, plain = total(n + 1), total(n + 2)
+        out_ref[taps : taps + 1, ch] = total(n)
+        out_ref[taps + 1 : taps + 2, ch] = along * scale_ref[:, ch]
+        out_ref[taps + 2 : taps + 3, ch] = plain * scale_ref[:, ch]
+        out_ref[taps + 3 : taps + 4, ch] = along * gain_ref[:, ch] + plain * shift_ref[:, ch]
 
 
 ANY = pl.BlockSpec(memory_space=pl.ANY)
@@ -293,12 +317,16 @@
     cap = tiles_dev // peers + 1
     slots, cbs = peers * cap, chans // LANES
     blocks = seq_grad.shape[0] // POS
-    part_out = cbs * cap * POS
-    part = part_out + 2
+    meta, extra = cbs * cap * POS, 4
+    part, back_part = meta + 2, meta + extra
+    holders = ROWS * cbs // 2
     f32, i32, bf16 = jnp.float32, jnp.int32, jnp.bfloat16
     shape = jax.ShapeDtypeStruct
     bias, gain, shift, scale = (v.reshape(1, chans) for v in (dw_bias, ln_gain, ln_shift, layer_scale))
-    grid = shape((cbs, POS, slots, LANES), f32)
+
+    def swap(v, axes):
+        return lax.all_to_all(v, axes, split_axis=0, concat_axis=0, tiled=True)
+
 
     ints = jnp.concatenate([tile_dest, tile_offset, sample_counts], 1)
     send, slot = call(
@@ -309,15 +337,19 @@
          pltpu.SMEM(ints.shape, i32), pltpu.SemaphoreType.DMA],
         (VMEM, SMEM),
     )(ints, tile_features.reshape(tiles_dev * POS, chans))
-    got = lax.all_to_all(send.reshape(peers, part // 2, 2, LANES), DP, split_axis=0, concat_axis=0, tiled=True)
-    x, u, f, sums, off = call(
+    got = swap(send.reshape(peers, part // 2, 2, LANES), DP)
+    data, ups, f, sums, off = call(
         functools.partial(conv_kernel, peers, cap, part),
         [VMEM] * 6,
-        (grid, grid, grid, shape((enc, 4 * POS, slots), f32), shape((slots,), i32)),
+        (
+            shape((peers * part, LANES), f32),
+            shape((cbs, slots * POS, LANES), f32),
+            shape((cbs, POS, slots, LANES), f32),
+            shape((enc, 4 * POS, slots), f32),
+            shape((slots,), i32),
+        ),
         [
-            pltpu.VMEM((peers * part, LANES), f32),
             pltpu.VMEM((cbs, (blocks + 1) * POS, LANES), f32),
-            pltpu.VMEM((cbs, slots * POS, LANES), f32),
             pltpu.VMEM((slots, LANES), f32),
             pltpu.VMEM((8, LANES), i32),
             pltpu.VMEM((8, LANES), f32),
@@ -327,30 +359,23 @@
         ],
         (VMEM, VMEM, VMEM, VMEM, SMEM),
     )(got.reshape(peers * part, LANES), seq_grad, dw_kernel, bias, gain, scale)
-    sums = lax.all_to_all(sums, ENC, split_axis=0, concat_axis=0, tiled=True)
-    outgoing, grads = call(
-        functools.partial(grad_kernel, peers, cap, width),
+    sums = swap(sums, ENC)
+    outgoing = call(
+        functools.partial(grad_kernel, peers, cap, part, extra, width),
         [VMEM] * 7,
-        (shape((peers * part_out, LANES), bf16), shape((ROWS, chans), f32)),
-        [pltpu.VMEM((slots, LANES), f32), pltpu.VMEM((peers * part_out, LANES), f32), pltpu.VMEM((ROWS, 8, chans), f32)],
-        (VMEM, VMEM),
-    )(sums, x, u, f, dw_kernel, gain, scale)
-    back = lax.all_to_all(outgoing.reshape(peers, part_out, LANES), DP, split_axis=0, concat_axis=0, tiled=True)
-    grads = lax.psum(lax.psum(grads, "y"), "zh")
-    inner = lax.axis_size("zl")
-    grads, back, off, sums = lax.optimization_barrier((grads, back, off, sums))
-    parts = lax.all_to_all(
-        jnp.broadcast_to(grads, (inner, ROWS, chans)), "zl", split_axis=0, concat_axis=0, tiled=True
-    )
-    tile_grads = call(
-        functools.partial(unpack_kernel, cap),
-        [SMEM, VMEM],
-        shape((tiles_dev * POS, chans), bf16),
-        [pltpu.VMEM((peers * part_out, LANES), f32), pltpu.VMEM((cbs, tiles_dev * POS, LANES), f32)],
+        shape((peers * back_part, LANES), bf16),
+        [
+            pltpu.VMEM((slots, LANES), f32),
+            pltpu.VMEM((peers * back_part, LANES), f32),
+            pltpu.VMEM((ROWS, 8, chans), f32),
+            pltpu.VMEM((holders, LANES), f32),
+            pltpu.VMEM((holders, LANES), f32),
+        ],
         VMEM,
-    )(slot, back.reshape(peers * part_out, LANES))
+    )(sums, data, ups, f, dw_kernel, gain, scale)
+    back = swap(outgoing.reshape(peers, back_part // 2, 2, LANES), DP).reshape(peers * back_part, LANES)
     vis = call(
-        functools.partial(token_kernel, peers, cap, width),
+        functools.partial(token_kernel, peers, cap, part, width),
         [SMEM] + [VMEM] * 6,
         shape((blocks * POS, chans), bf16),
         [
@@ -359,7 +384,16 @@
             pltpu.VMEM((cbs, (blocks + 1) * POS, LANES), f32),
         ],
         VMEM,
-    )(off, sums, x, f, gain, shift, scale)
+    )(off, sums, data, f, gain, shift, scale)
+    mine = call(functools.partial(total_kernel, meta, back_part), [VMEM], shape((peers, 2, LANES), f32), [], VMEM)(back)
+    parts = swap(mine, DP)
+    tile_grads = call(
+        functools.partial(unpack_kernel, cap, back_part),
+        [SMEM, VMEM],
+        shape((tiles_dev * POS, chans), bf16),
+        [pltpu.VMEM((peers * back_part, LANES), f32), pltpu.VMEM((cbs, tiles_dev * POS, LANES), f32)],
+        VMEM,
+    )(slot, back)
     param_grads = call(
         finish_kernel, [VMEM] * 4, shape((dw_kernel.shape[0] + 4, chans), f32), [], VMEM
     )(parts, gain, shift, scale)

time: 175 us -> 163 us (0.931)
  the two profiles are of different devices: /device:TPU:40 before, /device:TPU:2 now
where the time goes in v2:
time: 163 us; the launch traced here: 162 us
  blocking collectives  61.6 us (38%)
  waiting for transfers between devices  53.7 us (33%)
  starting transfers between devices  24.6 us (15%)
  Pallas kernels  17.1 us (10%)
  local copies, waits for them, and re-layouts  3.56 us (2%)
    all_to_all x2, blocking collectives, swap(): return lax.all_to_all(v, axes, split_axis=0, concat_axis=0, tiled=True)  61.6 us
    all_to_all x2, waiting for transfers between devices, swap(): return lax.all_to_all(v, axes, split_axis=0, concat_axis=0, tiled=True)  53.7 us
    all_to_all x2, starting transfers between devices, swap(): return lax.all_to_all(v, axes, split_axis=0, concat_axis=0, tiled=True)  24.6 us
    pallas_call x1, Pallas kernels, per_device(): call(functools.partial(conv_kernel, peers, cap, part), [VMEM] * 6, (shape...  4.56 us
    pallas_call x1, Pallas kernels, per_device(): call(functools.partial(grad_kernel, peers, cap, part, extra, width), [VME...  4.27 us
    pallas_call x1, Pallas kernels, per_device(): call(functools.partial(token_kernel, peers, cap, part, width), [SMEM] + [...  3.5 us
  transfers between devices with their start and end apart: 2, of which 2 were waited for; matrix products, arithmetic and copies ran while one was open for 1% of the time, Pallas kernels for 3%

profile of v2, /device:TPU:2, one launch (start us, length us, event | category | flops | bytes accessed | tf_op | source)
XLA Modules:
  0.0 162.1 jit_solution(17456898252466836385)
XLA Ops:
  0.6 0.0 copy-start.4
  0.6 0.0 copy-start.5
  0.7 0.0 copy-start.6
  0.7 0.0 copy-start.3
  0.7 0.0 copy-start.2
  0.7 1.2 reshape.36.tiles_ref
  1.9 0.8 pad_add_fusion.ints_hbm
  2.7 2.1 %shard_map.121 = (bf16[3200,128]{1,0:T(8,128)(2,1)}, s32[64]{0:T(128)S(1)}) custom-call(s32[1,136]{1,0:T(1,128)S(1)} %pad_add_fusion.ints_hbm, bf16[512,384]{1,0:T(8,128)(2,1)S(1)} %reshape.36.tiles_ref), custom_call_target="tpu_custom_call" | custom-call | tf_op jit(solution)/shard_map/pallas_call | solution.py:332
  4.8 18.7 %all-to-all-start = ((bf16[64,25,2,128]{3,2,1,0:T(2,128)(2,1)}), bf16[64,25,2,128]{3,2,1,0:T(2,128)(2,1)S(1)}, u32[]{:S(2)}, u32[]{:S(2)}) async-start(bf16[64,25,2,128]{3,2,1,0:T(2,128)(2,1)} %bitcast), calls=%async_computation | async-start | bytes 1638400 | tf_op jit(solution)/shard_map/all_to_all | solution.py:328
  23.6 0.0 copy-done.4
  23.6 0.0 copy-done.5
  23.6 0.0 copy-done.6
  23.6 45.4 %all-to-all-done = bf16[64,25,2,128]{3,2,1,0:T(2,128)(2,1)S(1)} async-done(((bf16[64,25,2,128]{3,2,1,0:T(2,128)(2,1)}), bf16[64,25,2,128]{3,2,1,0:T(2,128)(2,1)S(1)}, u32[]{:S(2)}, u32[]{:S(2)}) %all-to-all-start) | async-done | bytes 819232 | tf_op jit(solution)/shard_map/all_to_all | solution.py:328
  69.0 0.0 copy-done.3
  69.0 0.0 copy-done.2
  69.0 4.6 %shard_map.122 = (f32[3200,128]{1,0:T(8,128)S(1)}, f32[3,1024,128]{2,1,0:T(8,128)S(1)}, f32[3,8,128,128]{3,2,1,0:T(8,128)S(1)}, f32[8,32,128]{2,1,0:T(8,128)S(1)}, s32[128]{0:T(128)S(1)}) custom-call(bf16[3200,128]{1,0:T(8,128)(2,1)S(1)} %bitcast.7, bf16[1024,384]{1,0:T(8,128)(2,1)S(1)} %copy-done.2, f32[49,384]{1,0:T(8,128)S(1)} %copy-done.3, ...), custom_call_target="tpu_custom_call" | custom-call | tf_op jit(solution)/shard_map/pallas_call | solution.py:341
  73.6 0.0 copy-start
  73.6 9.3 %all_to_all.20.sums_ref = f32[8,32,128]{2,1,0:T(8,128)S(1)} all-to-all(f32[8,32,128]{2,1,0:T(8,128)S(1)} %get-tuple-element.12), channel_id=1, replica_groups=mesh['zh'=4,'zl'=4,'y'=4,'x'=4,'core'=2] {'x','core'}, dimensions={0} | all-to-all | bytes 262144 | tf_op jit(solution)/shard_map/all_to_all | solution.py:328
  82.9 4.3 %shard_map.124 = bf16[3328,128]{1,0:T(8,128)(2,1)S(1)} custom-call(f32[8,32,128]{2,1,0:T(8,128)S(1)} %all_to_all.20.sums_ref, f32[3200,128]{1,0:T(8,128)S(1)} %get-tuple-element.13.data_ref, f32[3,1024,128]{2,1,0:T(8,128)S(1)} %get-tuple-element.16.ups_ref, f32[3,8,128,128]{3,2,1,0:T(8,128)S(1)} %get-tuple-element.14.f_ref, f32[49,384]{1,0:T(8,128)S(1)} %copy-done.3, ...), custom_call_target="tpu_custom_call" | custom-call | tf_op jit(solution)/shard_map/pallas_call | solution.py:363
  87.2 0.0 copy-done
  87.2 0.0 copy-start.7
  87.2 52.3 %all_to_all.21 = bf16[64,26,2,128]{3,2,1,0:T(2,128)(2,1)S(1)} all-to-all(bf16[64,26,2,128]{3,2,1,0:T(2,128)(2,1)S(1)} %bitcast.6), channel_id=1, replica_groups=mesh['zh'=4,'zl'=4,'y'=4,'x'=4,'core'=2] {'zh','zl','y'}, dimensions={0} | all-to-all | bytes 1703936 | tf_op jit(solution)/shard_map/all_to_all | solution.py:328
  139.5 0.9 shard_map.126
  140.4 5.8 %all-to-all-start.3 = ((f32[64,2,128]{2,1,0:T(2,128)}), f32[64,2,128]{2,1,0:T(2,128)S(1)}, u32[]{:S(2)}, u32[]{:S(2)}) async-start(f32[64,2,128]{2,1,0:T(2,128)} %shard_map.126), calls=%async_computation.3 | async-start | bytes 131072 | tf_op jit(solution)/shard_map/all_to_all | solution.py:328
  146.2 0.0 copy-done.7
  146.3 0.0 copy-start.1
  146.3 1.4 copy-done.1
  147.7 3.5 %shard_map.123 = bf16[1024,384]{1,0:T(8,128)(2,1)} custom-call(s32[128]{0:T(128)S(1)} %get-tuple-element.11.off_ref, f32[8,32,128]{2,1,0:T(8,128)S(1)} %all_to_all.20.sums_ref, f32[3200,128]{1,0:T(8,128)S(1)} %get-tuple-element.13.data_ref, f32[3,8,128,128]{3,2,1,0:T(8,128)S(1)} %copy-done.1, f32[1,384]{1,0:T(1,128)S(1)} %reshape.40.gain_ref, ...), custom_call_target="tpu_custom_call" | custom-call | tf_op jit(solution)/shard_map/pallas_call | solution.py:377
  151.2 1.1 shard_map.125
  152.3 0.9 reshape.45
  153.2 8.3 %all-to-all-done.3.parts_ref = f32[64,2,128]{2,1,0:T(2,128)S(1)} async-done(((f32[64,2,128]{2,1,0:T(2,128)}), f32[64,2,128]{2,1,0:T(2,128)S(1)}, u32[]{:S(2)}, u32[]{:S(2)}) %all-to-all-start.3) | async-done | bytes 65568 | tf_op jit(solution)/shard_map/all_to_all | solution.py:328
  161.5 0.7 shard_map.127
  (4 shorter events, 0.0 us)
Async XLA Ops:
  0.6 22.9 %copy-start.4 = (f32[384]{0:T(512)S(1)}, f32[384]{0:T(512)}, u32[]{:S(2)}) copy-start(f32[384]{0:T(512)} %param.13) | copy-start | bytes 4612
  0.6 22.9 %copy-start.5 = (f32[384]{0:T(512)S(1)}, f32[384]{0:T(512)}, u32[]{:S(2)}) copy-start(f32[384]{0:T(512)} %param.15) | copy-start | bytes 4612
  0.7 23.0 %copy-start.6 = (f32[384]{0:T(512)S(1)}, f32[384]{0:T(512)}, u32[]{:S(2)}) copy-start(f32[384]{0:T(512)} %param.12) | copy-start | bytes 4612
  0.7 68.4 %copy-start.3 = (f32[49,384]{1,0:T(8,128)S(1)}, f32[49,384]{1,0:T(8,128)}, u32[]{:S(2)}) copy-start(f32[49,384]{1,0:T(8,128)} %kern_ref.3) | copy-start | bytes 225796
  0.7 68.4 %copy-start.2 = (bf16[1024,384]{1,0:T(8,128)(2,1)S(1)}, bf16[1024,384]{1,0:T(8,128)(2,1)}, u32[]{:S(2)}) copy-start(bf16[1024,384]{1,0:T(8,128)(2,1)} %seq_ref.1) | copy-start | bytes 2359300
  4.8 64.2 %all-to-all-start = ((bf16[64,25,2,128]{3,2,1,0:T(2,128)(2,1)}), bf16[64,25,2,128]{3,2,1,0:T(2,128)(2,1)S(1)}, u32[]{:S(2)}, u32[]{:S(2)}) async-start(bf16[64,25,2,128]{3,2,1,0:T(2,128)(2,1)} %bitcast), calls=%async_computation | async-start | bytes 1638400 | tf_op jit(solution)/shard_map/all_to_all | solution.py:328
  73.6 13.6 %copy-start = (f32[3,8,128,128]{3,2,1,0:T(8,128)}, f32[3,8,128,128]{3,2,1,0:T(8,128)S(1)}, u32[]{:S(2)}) copy-start(f32[3,8,128,128]{3,2,1,0:T(8,128)S(1)} %get-tuple-element.14.f_ref) | copy-start | bytes 4718596
  87.2 59.0 %copy-start.7 = (f32[384]{0:T(512)S(1)}, f32[384]{0:T(512)}, u32[]{:S(2)}) copy-start(f32[384]{0:T(512)} %param.14) | copy-start | bytes 4612
  140.4 21.1 %all-to-all-start.3 = ((f32[64,2,128]{2,1,0:T(2,128)}), f32[64,2,128]{2,1,0:T(2,128)S(1)}, u32[]{:S(2)}, u32[]{:S(2)}) async-start(f32[64,2,128]{2,1,0:T(2,128)} %shard_map.126), calls=%async_computation.3 | async-start | bytes 131072 | tf_op jit(solution)/shard_map/all_to_all | solution.py:328
  146.3 1.4 copy-start.1

commit v3 on v2

--- a/solution.py
+++ b/solution.py
@@ -13,6 +13,7 @@
 POS = HGT * WID
 LANES = 128
 DP = ("zh", "zl", "y")
+NEAR = ("zl", "y")
 ENC = ("x", "core")
 VMEM_LIMIT = 16 * 1024 * 1024
 
@@ -144,11 +145,11 @@
     return jnp.concatenate(rows, 0).T
 
 
-def grad_kernel(peers, cap, part, extra, width, sums_ref, data_ref, ups_ref, f_ref, kern_ref, gain_ref, scale_ref,
-                out_ref, stats, data, acc, even, odd):
+def grad_kernel(peers, near, cap, part, each, width, sums_ref, data_ref, ups_ref, f_ref, kern_ref, gain_ref, scale_ref,
+                out_ref, stats, data, acc, partial):
     cbs = f_ref.shape[0]
     meta = cbs * cap * POS
-    back = meta + extra
+    back = meta + 2 * each
     stats[...] = stats_columns(sums_ref, width)
     acc[...] = jnp.zeros_like(acc)
     for r in range(cap):
@@ -197,16 +198,14 @@
     for row in range(ROWS):
         for cb in range(cbs):
             v = row * cbs + cb
-            half = even if v % 2 == 0 else odd
-            half[v // 2 : v // 2 + 1, :] = jnp.sum(acc[row, :, cb * LANES : (cb + 1) * LANES], 0, keepdims=True)
-    holders = even.shape[0]
-    for i, half in enumerate((even, odd)):
-        sums = half[...]
+            partial[v : v + 1, :] = jnp.sum(acc[row, :, cb * LANES : (cb + 1) * LANES], 0, keepdims=True)
+    partial[ROWS * cbs :, :] = jnp.zeros((each * near - ROWS * cbs, LANES), jnp.float32)
+    for i in range(each):
+        sums = partial[pl.ds(i, near, stride=each), :]
         high = sums.astype(jnp.bfloat16).astype(jnp.float32)
-        for j, v in ((i, high), (i + 2, sums - high)):
-            data[pl.ds(meta + j, holders, stride=back), :] = v
-    for j in range(extra):
-        data[pl.ds(holders * back + meta + j, peers - holders, stride=back), :] = jnp.zeros((peers - holders, LANES), jnp.float32)
+        for j, v in ((i, high), (i + each, sums - high)):
+            for far in range(peers // near):
+                data[pl.ds(far * near * back + meta + j, near, stride=back), :] = v
     out_ref[...] = data[...].astype(jnp.bfloat16)
 
 
@@ -243,15 +242,15 @@
         vis_ref[:, cb * LANES : (cb + 1) * LANES] = data[cb, 0 : vis_ref.shape[0], :].astype(jnp.bfloat16)
 
 
-def total_kernel(meta, back, back_ref, out_ref):
-    peers = out_ref.shape[0]
+def total_kernel(meta, each, back_ref, out_ref):
+    near, high, _ = out_ref.shape
     rows = back_ref.shape[0]
-    at = lax.rem(lax.broadcasted_iota(jnp.int32, (8, rows), 1), back) - meta
-    which = lax.broadcasted_iota(jnp.int32, (8, rows), 0)
-    pick = jnp.where((at == which) | (at == which + 2), 1.0, 0.0)
-    pick = jnp.where(which < 2, pick, 0.0).astype(jnp.bfloat16)
-    total = jnp.dot(pick, back_ref[...], preferred_element_type=jnp.float32)[0:2]
-    out_ref[...] = jnp.broadcast_to(total[None], (peers, 2, LANES))
+    at = lax.rem(lax.broadcasted_iota(jnp.int32, (high, rows), 1), meta + 2 * each) - meta
+    which = lax.broadcasted_iota(jnp.int32, (high, rows), 0)
+    pick = jnp.where((which < each) & ((at == which) | (at == which + each)), 1.0, 0.0).astype(jnp.bfloat16)
+    total = jnp.dot(pick, back_ref[...], preferred_element_type=jnp.float32)
+    for i in range(near):
+        out_ref[i] = total
 
 
 def unpack_kernel(cap, part, slot_ref, back_ref, out_ref, data, rows):
@@ -272,7 +271,7 @@
         out_ref[:, cb * LANES : (cb + 1) * LANES] = rows[cb].astype(jnp.bfloat16)
 
 
-def finish_kernel(parts_ref, gain_ref, shift_ref, scale_ref, out_ref):
+def finish_kernel(each, parts_ref, gain_ref, shift_ref, scale_ref, out_ref):
     out_ref[...] = jnp.zeros_like(out_ref)
     n, taps = len(USED), out_ref.shape[0] - 4
     cbs = out_ref.shape[1] // LANES
@@ -281,7 +280,7 @@
 
         def total(i):
             v = i * cbs + cb
-            return parts_ref[v // 2, v % 2 : v % 2 + 1, :]
+            return parts_ref[v // each, v % each : v % each + 1, :]
 
         for i, tap in enumerate(USED):
             out_ref[tap : tap + 1, ch] = total(i)
@@ -317,9 +316,10 @@
     cap = tiles_dev // peers + 1
     slots, cbs = peers * cap, chans // LANES
     blocks = seq_grad.shape[0] // POS
-    meta, extra = cbs * cap * POS, 4
-    part, back_part = meta + 2, meta + extra
-    holders = ROWS * cbs // 2
+    near = lax.axis_size(NEAR)
+    each = -(-ROWS * cbs // near)
+    meta = cbs * cap * POS
+    part, back_part = meta + 2, meta + 2 * each
     f32, i32, bf16 = jnp.float32, jnp.int32, jnp.bfloat16
     shape = jax.ShapeDtypeStruct
     bias, gain, shift, scale = (v.reshape(1, chans) for v in (dw_bias, ln_gain, ln_shift, layer_scale))
@@ -361,15 +361,14 @@
     )(got.reshape(peers * part, LANES), seq_grad, dw_kernel, bias, gain, scale)
     sums = swap(sums, ENC)
     outgoing = call(
-        functools.partial(grad_kernel, peers, cap, part, extra, width),
+        functools.partial(grad_kernel, peers, near, cap, part, each, width),
         [VMEM] * 7,
         shape((peers * back_part, LANES), bf16),
         [
             pltpu.VMEM((slots, LANES), f32),
             pltpu.VMEM((peers * back_part, LANES), f32),
             pltpu.VMEM((ROWS, 8, chans), f32),
-            pltpu.VMEM((holders, LANES), f32),
-            pltpu.VMEM((holders, LANES), f32),
+            pltpu.VMEM((near * each, LANES), f32),
         ],
         VMEM,
     )(sums, data, ups, f, dw_kernel, gain, scale)
@@ -385,8 +384,9 @@
         ],
         VMEM,
     )(off, sums, data, f, gain, shift, scale)
-    mine = call(functools.partial(total_kernel, meta, back_part), [VMEM], shape((peers, 2, LANES), f32), [], VMEM)(back)
-    parts = swap(mine, DP)
+    back, vis = lax.optimization_barrier((back, vis))
+    mine = call(functools.partial(total_kernel, meta, each), [VMEM], shape((near, 8, LANES), f32), [], VMEM)(back)
+    parts = swap(mine, NEAR)
     tile_grads = call(
         functools.partial(unpack_kernel, cap, back_part),
         [SMEM, VMEM],
@@ -395,7 +395,7 @@
         VMEM,
     )(slot, back)
     param_grads = call(
-        finish_kernel, [VMEM] * 4, shape((dw_kernel.shape[0] + 4, chans), f32), [], VMEM
+        functools.partial(finish_kernel, each), [VMEM] * 4, shape((dw_kernel.shape[0] + 4, chans), f32), [], VMEM
     )(parts, gain, shift, scale)
     return vis, tile_grads.reshape(tile_features.shape), param_grads
 

time: 163 us -> 160 us (0.982)
  blocking collectives: 61.6 us -> 9.31 us
  waiting for transfers between devices: 53.7 us -> 97.7 us
  starting transfers between devices: 24.6 us -> 29.2 us
    all_to_all x2 -> x1, blocking collectives: 61.6 us -> 9.31 us  [swap(): return lax.all_to_all(v, axes, split_axis=0, concat_axis=0, tiled=True)]
    all_to_all x2 -> x3, waiting for transfers between devices: 53.7 us -> 97.7 us  [swap(): return lax.all_to_all(v, axes, split_axis=0, concat_axis=0, tiled=True)]
    all_to_all x2 -> x3, starting transfers between devices: 24.6 us -> 29.2 us  [swap(): return lax.all_to_all(v, axes, split_axis=0, concat_axis=0, tiled=True)]
  transfers between devices with their start and end apart: 2 -> 3, of which waited for: 2 -> 3; matrix products, arithmetic and copies ran while one was open for 1% -> 1% of each run, Pallas kernels for 3% -> 3%
where the time goes in v3:
time: 160 us; the launch traced here: 159 us
  waiting for transfers between devices  97.7 us (61%)
  starting transfers between devices  29.2 us (18%)
  Pallas kernels  18.1 us (11%)
  blocking collectives  9.31 us (6%)
  local copies, waits for them, and re-layouts  3.56 us (2%)
    all_to_all x3, waiting for transfers between devices, swap(): return lax.all_to_all(v, axes, split_axis=0, concat_axis=0, tiled=True)  97.7 us
    all_to_all x3, starting transfers between devices, swap(): return lax.all_to_all(v, axes, split_axis=0, concat_axis=0, tiled=True)  29.2 us
    all_to_all x1, blocking collectives, swap(): return lax.all_to_all(v, axes, split_axis=0, concat_axis=0, tiled=True)  9.31 us
    pallas_call x1, Pallas kernels, per_device(): call(functools.partial(grad_kernel, peers, near, cap, part, each, width),...  5.23 us
    pallas_call x1, Pallas kernels, per_device(): call(functools.partial(conv_kernel, peers, cap, part), [VMEM] * 6, (shape...  4.56 us
    pallas_call x1, Pallas kernels, per_device(): call(functools.partial(token_kernel, peers, cap, part, width), [SMEM] + [...  3.5 us
  transfers between devices with their start and end apart: 3, of which 3 were waited for; matrix products, arithmetic and copies ran while one was open for 1% of the time, Pallas kernels for 3%

profile of v3, /device:TPU:2, one launch (start us, length us, event | category | flops | bytes accessed | tf_op | source)
XLA Modules:
  0.0 159.4 jit_solution(17106661601953783136)
XLA Ops:
  0.6 0.0 copy-start.4
  0.6 0.0 copy-start.5
  0.7 0.0 copy-start.6
  0.7 0.0 copy-start.2
  0.7 0.0 copy-start.3
  0.7 1.2 reshape.36.tiles_ref
  1.9 0.8 pad_add_fusion.ints_hbm
  2.7 2.1 %shard_map.121 = (bf16[3200,128]{1,0:T(8,128)(2,1)}, s32[64]{0:T(128)S(1)}) custom-call(s32[1,136]{1,0:T(1,128)S(1)} %pad_add_fusion.ints_hbm, bf16[512,384]{1,0:T(8,128)(2,1)S(1)} %reshape.36.tiles_ref), custom_call_target="tpu_custom_call" | custom-call | tf_op jit(solution)/shard_map/pallas_call | solution.py:332
  4.8 18.7 %all-to-all-start = ((bf16[64,25,2,128]{3,2,1,0:T(2,128)(2,1)}), bf16[64,25,2,128]{3,2,1,0:T(2,128)(2,1)S(1)}, u32[]{:S(2)}, u32[]{:S(2)}) async-start(bf16[64,25,2,128]{3,2,1,0:T(2,128)(2,1)} %bitcast), calls=%async_computation | async-start | bytes 1638400 | tf_op jit(solution)/shard_map/all_to_all | solution.py:328
  23.6 0.0 copy-done.4
  23.6 0.0 copy-done.5
  23.6 0.0 copy-done.6
  23.6 45.4 %all-to-all-done = bf16[64,25,2,128]{3,2,1,0:T(2,128)(2,1)S(1)} async-done(((bf16[64,25,2,128]{3,2,1,0:T(2,128)(2,1)}), bf16[64,25,2,128]{3,2,1,0:T(2,128)(2,1)S(1)}, u32[]{:S(2)}, u32[]{:S(2)}) %all-to-all-start) | async-done | bytes 819232 | tf_op jit(solution)/shard_map/all_to_all | solution.py:328
  69.0 0.0 copy-done.2
  69.0 0.0 copy-done.3
  69.0 4.6 %shard_map.122 = (f32[3200,128]{1,0:T(8,128)S(1)}, f32[3,1024,128]{2,1,0:T(8,128)S(1)}, f32[3,8,128,128]{3,2,1,0:T(8,128)S(1)}, f32[8,32,128]{2,1,0:T(8,128)S(1)}, s32[128]{0:T(128)S(1)}) custom-call(bf16[3200,128]{1,0:T(8,128)(2,1)S(1)} %bitcast.6, bf16[1024,384]{1,0:T(8,128)(2,1)S(1)} %copy-done.2, f32[49,384]{1,0:T(8,128)S(1)} %copy-done.3, ...), custom_call_target="tpu_custom_call" | custom-call | tf_op jit(solution)/shard_map/pallas_call | solution.py:341
  73.6 0.0 copy-start
  73.6 9.3 %all_to_all.20.sums_ref = f32[8,32,128]{2,1,0:T(8,128)S(1)} all-to-all(f32[8,32,128]{2,1,0:T(8,128)S(1)} %get-tuple-element.13), channel_id=1, replica_groups=mesh['zh'=4,'zl'=4,'y'=4,'x'=4,'core'=2] {'x','core'}, dimensions={0} | all-to-all | bytes 262144 | tf_op jit(solution)/shard_map/all_to_all | solution.py:328
  82.9 5.2 %shard_map.123 = bf16[3712,128]{1,0:T(8,128)(2,1)} custom-call(f32[8,32,128]{2,1,0:T(8,128)S(1)} %all_to_all.20.sums_ref, f32[3200,128]{1,0:T(8,128)S(1)} %get-tuple-element.14.data_ref, f32[3,1024,128]{2,1,0:T(8,128)S(1)} %get-tuple-element.15.ups_ref, f32[3,8,128,128]{3,2,1,0:T(8,128)S(1)} %get-tuple-element.16.f_ref, f32[49,384]{1,0:T(8,128)S(1)} %copy-done.3, ...), custom_call_target="tpu_custom_call" | custom-call | tf_op jit(solution)/shard_map/pallas_call | solution.py:363
  88.1 0.0 copy-done
  88.1 0.0 copy-start.7
  88.1 6.0 %all-to-all-start.2 = ((bf16[64,29,2,128]{3,2,1,0:T(2,128)(2,1)}), bf16[64,29,2,128]{3,2,1,0:T(2,128)(2,1)S(1)}, u32[]{:S(2)}, u32[]{:S(2)}) async-start(bf16[64,29,2,128]{3,2,1,0:T(2,128)(2,1)} %bitcast.2), calls=%async_computation.2 | async-start | bytes 1900544 | tf_op jit(solution)/shard_map/all_to_all | solution.py:328
  94.1 0.0 copy-done.7
  94.1 0.0 copy-start.1
  94.1 1.4 copy-done.1
  95.5 3.5 %shard_map.124 = bf16[1024,384]{1,0:T(8,128)(2,1)} custom-call(s32[128]{0:T(128)S(1)} %get-tuple-element.17.off_ref, f32[8,32,128]{2,1,0:T(8,128)S(1)} %all_to_all.20.sums_ref, f32[3200,128]{1,0:T(8,128)S(1)} %get-tuple-element.14.data_ref, f32[3,8,128,128]{3,2,1,0:T(8,128)S(1)} %copy-done.1, f32[1,384]{1,0:T(1,128)S(1)} %reshape.40.gain_ref, ...), custom_call_target="tpu_custom_call" | custom-call | tf_op jit(solution)/shard_map/pallas_call | solution.py:376
  99.0 46.0 %all-to-all-done.2 = bf16[64,29,2,128]{3,2,1,0:T(2,128)(2,1)S(1)} async-done(((bf16[64,29,2,128]{3,2,1,0:T(2,128)(2,1)}), bf16[64,29,2,128]{3,2,1,0:T(2,128)(2,1)S(1)}, u32[]{:S(2)}, u32[]{:S(2)}) %all-to-all-start.2) | async-done | bytes 950304 | tf_op jit(solution)/shard_map/all_to_all | solution.py:328
  145.0 0.9 shard_map.126
  145.9 4.4 %all-to-all-start.3 = ((f32[16,8,128]{2,1,0:T(8,128)}), f32[16,8,128]{2,1,0:T(8,128)S(1)}, u32[]{:S(2)}, u32[]{:S(2)}) async-start(f32[16,8,128]{2,1,0:T(8,128)} %shard_map.126), calls=%async_computation.3 | async-start | bytes 131072 | tf_op jit(solution)/shard_map/all_to_all | solution.py:328
  150.3 1.1 shard_map.125
  151.5 0.9 reshape.45
  152.4 6.4 %all-to-all-done.3.parts_ref = f32[16,8,128]{2,1,0:T(8,128)S(1)} async-done(((f32[16,8,128]{2,1,0:T(8,128)}), f32[16,8,128]{2,1,0:T(8,128)S(1)}, u32[]{:S(2)}, u32[]{:S(2)}) %all-to-all-start.3) | async-done | bytes 65568 | tf_op jit(solution)/shard_map/all_to_all | solution.py:328
  158.7 0.7 shard_map.127
  (4 shorter events, 0.0 us)
Async XLA Ops:
  0.6 22.9 %copy-start.4 = (f32[384]{0:T(512)S(1)}, f32[384]{0:T(512)}, u32[]{:S(2)}) copy-start(f32[384]{0:T(512)} %param.12) | copy-start | bytes 4612
  0.6 22.9 %copy-start.5 = (f32[384]{0:T(512)S(1)}, f32[384]{0:T(512)}, u32[]{:S(2)}) copy-start(f32[384]{0:T(512)} %param.13) | copy-start | bytes 4612
  0.7 22.9 %copy-start.6 = (f32[384]{0:T(512)S(1)}, f32[384]{0:T(512)}, u32[]{:S(2)}) copy-start(f32[384]{0:T(512)} %param.15) | copy-start | bytes 4612
  0.7 68.4 %copy-start.2 = (bf16[1024,384]{1,0:T(8,128)(2,1)S(1)}, bf16[1024,384]{1,0:T(8,128)(2,1)}, u32[]{:S(2)}) copy-start(bf16[1024,384]{1,0:T(8,128)(2,1)} %seq_ref.1) | copy-start | bytes 2359300
  0.7 68.3 %copy-start.3 = (f32[49,384]{1,0:T(8,128)S(1)}, f32[49,384]{1,0:T(8,128)}, u32[]{:S(2)}) copy-start(f32[49,384]{1,0:T(8,128)} %kern_ref.3) | copy-start | bytes 225796
  4.8 64.2 %all-to-all-start = ((bf16[64,25,2,128]{3,2,1,0:T(2,128)(2,1)}), bf16[64,25,2,128]{3,2,1,0:T(2,128)(2,1)S(1)}, u32[]{:S(2)}, u32[]{:S(2)}) async-start(bf16[64,25,2,128]{3,2,1,0:T(2,128)(2,1)} %bitcast), calls=%async_computation | async-start | bytes 1638400 | tf_op jit(solution)/shard_map/all_to_all | solution.py:328
  73.6 14.5 %copy-start = (f32[3,8,128,128]{3,2,1,0:T(8,128)}, f32[3,8,128,128]{3,2,1,0:T(8,128)S(1)}, u32[]{:S(2)}) copy-start(f32[3,8,128,128]{3,2,1,0:T(8,128)S(1)} %get-tuple-element.16.f_ref) | copy-start | bytes 4718596
  88.1 6.0 %copy-start.7 = (f32[384]{0:T(512)S(1)}, f32[384]{0:T(512)}, u32[]{:S(2)}) copy-start(f32[384]{0:T(512)} %param.14) | copy-start | bytes 4612
  88.1 56.9 %all-to-all-start.2 = ((bf16[64,29,2,128]{3,2,1,0:T(2,128)(2,1)}), bf16[64,29,2,128]{3,2,1,0:T(2,128)(2,1)S(1)}, u32[]{:S(2)}, u32[]{:S(2)}) async-start(bf16[64,29,2,128]{3,2,1,0:T(2,128)(2,1)} %bitcast.2), calls=%async_computation.2 | async-start | bytes 1900544 | tf_op jit(solution)/shard_map/all_to_all | solution.py:328
  94.1 1.4 copy-start.1
  145.9 12.9 %all-to-all-start.3 = ((f32[16,8,128]{2,1,0:T(8,128)}), f32[16,8,128]{2,1,0:T(8,128)S(1)}, u32[]{:S(2)}, u32[]{:S(2)}) async-start(f32[16,8,128]{2,1,0:T(8,128)} %shard_map.126), calls=%async_computation.3 | async-start | bytes 131072 | tf_op jit(solution)/shard_map/all_to_all | solution.py:328

commit v4 on v3

--- a/solution.py
+++ b/solution.py
@@ -98,7 +98,7 @@
                 )
             return c
 
-        lax.fori_loop(0, peers, fetch, 0, unroll=8)
+        lax.fori_loop(0, peers, fetch, 0, unroll=32)
     lane = lax.broadcasted_iota(jnp.int32, (8, LANES), 1)
     for r in range(cap):
 
@@ -126,7 +126,7 @@
             cols[here, :] = out
             return c
 
-        lax.fori_loop(0, peers // 8, body, 0)
+        lax.fori_loop(0, peers // 8, body, 0, unroll=8)
     total = cols[...].T[0 : 4 * POS]
     for i in range(sums_ref.shape[0]):
         sums_ref[i] = total
@@ -140,8 +140,10 @@
     inv = lax.rsqrt(jnp.maximum(sums[POS : 2 * POS] / width - center * center, 0.0) + EPS)
     first = sums[2 * POS : 3 * POS]
     second = inv * (sums[3 * POS : 4 * POS] - center * first)
+    slope = -(inv * inv) * (second / width)
+    base = -inv * (first / width) - slope * center
     slots = sums.shape[1]
-    rows = [center, inv, first / width, second / width, jnp.zeros((LANES - 4 * POS, slots), jnp.float32)]
+    rows = [center, inv, base, slope, jnp.zeros((LANES - 4 * POS, slots), jnp.float32)]
     return jnp.concatenate(rows, 0).T
 
 
@@ -168,12 +170,14 @@
                 for p in range(POS):
                     col = [st[:, k * POS + p : k * POS + p + 1] for k in range(4)]
                     u = ups_ref[cb, pl.ds((r * peers + b * 8) * POS + p, 8, stride=POS), :]
-                    n = (f_ref[cb, p, here, :] - col[0]) * col[1]
-                    d = col[1] * (u * (scale_ref[:, ch] * gain_ref[:, ch]) - col[2] - n * col[3])
+                    f = f_ref[cb, p, here, :]
+                    w = u * col[1]
+                    d = w * (scale_ref[:, ch] * gain_ref[:, ch]) + (f * col[3] + col[2])
+                    along = w * (f - col[0])
                     df.append(d)
                     us.append(u)
                     xs.append(data_ref[pl.ds(b * 8 * part + cb * cap * POS + r * POS + p, 8, stride=part), :])
-                    a_sum = u * n if p == 0 else a_sum + u * n
+                    a_sum = along if p == 0 else a_sum + along
                     b_sum = u if p == 0 else b_sum + u
                     d_sum = d if p == 0 else d_sum + d
                 taps = {}
@@ -194,7 +198,7 @@
                     data[pl.ds(b * 8 * back + cb * cap * POS + r * POS + q, 8, stride=back), :] = t
             return c
 
-        lax.fori_loop(0, peers // 8, body, 0)
+        lax.fori_loop(0, peers // 8, body, 0, unroll=8)
     for row in range(ROWS):
         for cb in range(cbs):
             v = row * cbs + cb

time: 160 us -> 157 us (0.981)
  Pallas kernels: 18.1 us -> 15.1 us
    pallas_call x1, Pallas kernels: 4.56 us -> 2.64 us  [per_device(): call(functools.partial(conv_kernel, peers, cap, part), [VMEM] * 6, (shape...]
where the time goes in v4:
time: 157 us; the launch traced here: 156 us
  waiting for transfers between devices  97.7 us (62%)
  starting transfers between devices  29.2 us (19%)
  Pallas kernels  15.1 us (10%)
  blocking collectives  9.31 us (6%)
  local copies, waits for them, and re-layouts  3.56 us (2%)
    all_to_all x3, waiting for transfers between devices, swap(): return lax.all_to_all(v, axes, split_axis=0, concat_axis=0, tiled=True)  97.7 us
    all_to_all x3, starting transfers between devices, swap(): return lax.all_to_all(v, axes, split_axis=0, concat_axis=0, tiled=True)  29.2 us
    all_to_all x1, blocking collectives, swap(): return lax.all_to_all(v, axes, split_axis=0, concat_axis=0, tiled=True)  9.31 us
    pallas_call x1, Pallas kernels, per_device(): call(functools.partial(grad_kernel, peers, near, cap, part, each, width),...  4.15 us
    pallas_call x1, Pallas kernels, per_device(): call(functools.partial(token_kernel, peers, cap, part, width), [SMEM] + [...  3.5 us
  transfers between devices with their start and end apart: 3, of which 3 were waited for; matrix products, arithmetic and copies ran while one was open for 1% of the time, Pallas kernels for 3%

profile of v4, /device:TPU:2, one launch (start us, length us, event | category | flops | bytes accessed | tf_op | source)
XLA Modules:
  0.0 156.4 jit_solution(18409823167993817009)
XLA Ops:
  0.6 0.0 copy-start.4
  0.6 0.0 copy-start.5
  0.7 0.0 copy-start.6
  0.7 0.0 copy-start.2
  0.7 0.0 copy-start.3
  0.7 1.2 reshape.36.tiles_ref
  1.9 0.8 pad_add_fusion.ints_hbm
  2.7 2.1 %shard_map.121 = (bf16[3200,128]{1,0:T(8,128)(2,1)}, s32[64]{0:T(128)S(1)}) custom-call(s32[1,136]{1,0:T(1,128)S(1)} %pad_add_fusion.ints_hbm, bf16[512,384]{1,0:T(8,128)(2,1)S(1)} %reshape.36.tiles_ref), custom_call_target="tpu_custom_call" | custom-call | tf_op jit(solution)/shard_map/pallas_call | solution.py:336
  4.8 18.7 %all-to-all-start = ((bf16[64,25,2,128]{3,2,1,0:T(2,128)(2,1)}), bf16[64,25,2,128]{3,2,1,0:T(2,128)(2,1)S(1)}, u32[]{:S(2)}, u32[]{:S(2)}) async-start(bf16[64,25,2,128]{3,2,1,0:T(2,128)(2,1)} %bitcast), calls=%async_computation | async-start | bytes 1638400 | tf_op jit(solution)/shard_map/all_to_all | solution.py:332
  23.6 0.0 copy-done.4
  23.6 0.0 copy-done.5
  23.6 0.0 copy-done.6
  23.6 45.4 %all-to-all-done = bf16[64,25,2,128]{3,2,1,0:T(2,128)(2,1)S(1)} async-done(((bf16[64,25,2,128]{3,2,1,0:T(2,128)(2,1)}), bf16[64,25,2,128]{3,2,1,0:T(2,128)(2,1)S(1)}, u32[]{:S(2)}, u32[]{:S(2)}) %all-to-all-start) | async-done | bytes 819232 | tf_op jit(solution)/shard_map/all_to_all | solution.py:332
  69.0 0.0 copy-done.2
  69.0 0.0 copy-done.3
  69.0 2.6 %shard_map.122 = (f32[3200,128]{1,0:T(8,128)S(1)}, f32[3,1024,128]{2,1,0:T(8,128)S(1)}, f32[3,8,128,128]{3,2,1,0:T(8,128)S(1)}, f32[8,32,128]{2,1,0:T(8,128)S(1)}, s32[128]{0:T(128)S(1)}) custom-call(bf16[3200,128]{1,0:T(8,128)(2,1)S(1)} %bitcast.6, bf16[1024,384]{1,0:T(8,128)(2,1)S(1)} %copy-done.2, f32[49,384]{1,0:T(8,128)S(1)} %copy-done.3, ...), custom_call_target="tpu_custom_call" | custom-call | tf_op jit(solution)/shard_map/pallas_call | solution.py:345
  71.7 0.0 copy-start
  71.7 9.3 %all_to_all.20.sums_ref = f32[8,32,128]{2,1,0:T(8,128)S(1)} all-to-all(f32[8,32,128]{2,1,0:T(8,128)S(1)} %get-tuple-element.13), channel_id=1, replica_groups=mesh['zh'=4,'zl'=4,'y'=4,'x'=4,'core'=2] {'x','core'}, dimensions={0} | all-to-all | bytes 262144 | tf_op jit(solution)/shard_map/all_to_all | solution.py:332
  81.0 4.2 %shard_map.123 = bf16[3712,128]{1,0:T(8,128)(2,1)} custom-call(f32[8,32,128]{2,1,0:T(8,128)S(1)} %all_to_all.20.sums_ref, f32[3200,128]{1,0:T(8,128)S(1)} %get-tuple-element.14.data_ref, f32[3,1024,128]{2,1,0:T(8,128)S(1)} %get-tuple-element.15.ups_ref, f32[3,8,128,128]{3,2,1,0:T(8,128)S(1)} %get-tuple-element.16.f_ref, f32[49,384]{1,0:T(8,128)S(1)} %copy-done.3, ...), custom_call_target="tpu_custom_call" | custom-call | tf_op jit(solution)/shard_map/pallas_call | solution.py:367
  85.1 0.0 copy-done
  85.1 0.0 copy-start.7
  85.1 6.0 %all-to-all-start.2 = ((bf16[64,29,2,128]{3,2,1,0:T(2,128)(2,1)}), bf16[64,29,2,128]{3,2,1,0:T(2,128)(2,1)S(1)}, u32[]{:S(2)}, u32[]{:S(2)}) async-start(bf16[64,29,2,128]{3,2,1,0:T(2,128)(2,1)} %bitcast.2), calls=%async_computation.2 | async-start | bytes 1900544 | tf_op jit(solution)/shard_map/all_to_all | solution.py:332
  91.1 0.0 copy-done.7
  91.1 0.0 copy-start.1
  91.1 1.4 copy-done.1
  92.5 3.5 %shard_map.124 = bf16[1024,384]{1,0:T(8,128)(2,1)} custom-call(s32[128]{0:T(128)S(1)} %get-tuple-element.17.off_ref, f32[8,32,128]{2,1,0:T(8,128)S(1)} %all_to_all.20.sums_ref, f32[3200,128]{1,0:T(8,128)S(1)} %get-tuple-element.14.data_ref, f32[3,8,128,128]{3,2,1,0:T(8,128)S(1)} %copy-done.1, f32[1,384]{1,0:T(1,128)S(1)} %reshape.40.gain_ref, ...), custom_call_target="tpu_custom_call" | custom-call | tf_op jit(solution)/shard_map/pallas_call | solution.py:380
  96.0 46.0 %all-to-all-done.2 = bf16[64,29,2,128]{3,2,1,0:T(2,128)(2,1)S(1)} async-done(((bf16[64,29,2,128]{3,2,1,0:T(2,128)(2,1)}), bf16[64,29,2,128]{3,2,1,0:T(2,128)(2,1)S(1)}, u32[]{:S(2)}, u32[]{:S(2)}) %all-to-all-start.2) | async-done | bytes 950304 | tf_op jit(solution)/shard_map/all_to_all | solution.py:332
  142.0 0.9 shard_map.126
  142.9 4.4 %all-to-all-start.3 = ((f32[16,8,128]{2,1,0:T(8,128)}), f32[16,8,128]{2,1,0:T(8,128)S(1)}, u32[]{:S(2)}, u32[]{:S(2)}) async-start(f32[16,8,128]{2,1,0:T(8,128)} %shard_map.126), calls=%async_computation.3 | async-start | bytes 131072 | tf_op jit(solution)/shard_map/all_to_all | solution.py:332
  147.3 1.1 shard_map.125
  148.5 0.9 reshape.45
  149.4 6.4 %all-to-all-done.3.parts_ref = f32[16,8,128]{2,1,0:T(8,128)S(1)} async-done(((f32[16,8,128]{2,1,0:T(8,128)}), f32[16,8,128]{2,1,0:T(8,128)S(1)}, u32[]{:S(2)}, u32[]{:S(2)}) %all-to-all-start.3) | async-done | bytes 65568 | tf_op jit(solution)/shard_map/all_to_all | solution.py:332
  155.7 0.7 shard_map.127
  (4 shorter events, 0.0 us)
Async XLA Ops:
  0.6 22.9 %copy-start.4 = (f32[384]{0:T(512)S(1)}, f32[384]{0:T(512)}, u32[]{:S(2)}) copy-start(f32[384]{0:T(512)} %param.12) | copy-start | bytes 4612
  0.6 22.9 %copy-start.5 = (f32[384]{0:T(512)S(1)}, f32[384]{0:T(512)}, u32[]{:S(2)}) copy-start(f32[384]{0:T(512)} %param.13) | copy-start | bytes 4612
  0.7 22.9 %copy-start.6 = (f32[384]{0:T(512)S(1)}, f32[384]{0:T(512)}, u32[]{:S(2)}) copy-start(f32[384]{0:T(512)} %param.15) | copy-start | bytes 4612
  0.7 68.4 %copy-start.2 = (bf16[1024,384]{1,0:T(8,128)(2,1)S(1)}, bf16[1024,384]{1,0:T(8,128)(2,1)}, u32[]{:S(2)}) copy-start(bf16[1024,384]{1,0:T(8,128)(2,1)} %seq_ref.1) | copy-start | bytes 2359300
  0.7 68.3 %copy-start.3 = (f32[49,384]{1,0:T(8,128)S(1)}, f32[49,384]{1,0:T(8,128)}, u32[]{:S(2)}) copy-start(f32[49,384]{1,0:T(8,128)} %kern_ref.3) | copy-start | bytes 225796
  4.8 64.2 %all-to-all-start = ((bf16[64,25,2,128]{3,2,1,0:T(2,128)(2,1)}), bf16[64,25,2,128]{3,2,1,0:T(2,128)(2,1)S(1)}, u32[]{:S(2)}, u32[]{:S(2)}) async-start(bf16[64,25,2,128]{3,2,1,0:T(2,128)(2,1)} %bitcast), calls=%async_computation | async-start | bytes 1638400 | tf_op jit(solution)/shard_map/all_to_all | solution.py:332
  71.7 13.5 %copy-start = (f32[3,8,128,128]{3,2,1,0:T(8,128)}, f32[3,8,128,128]{3,2,1,0:T(8,128)S(1)}, u32[]{:S(2)}) copy-start(f32[3,8,128,128]{3,2,1,0:T(8,128)S(1)} %get-tuple-element.16.f_ref) | copy-start | bytes 4718596
  85.1 6.0 %copy-start.7 = (f32[384]{0:T(512)S(1)}, f32[384]{0:T(512)}, u32[]{:S(2)}) copy-start(f32[384]{0:T(512)} %param.14) | copy-start | bytes 4612
  85.1 56.9 %all-to-all-start.2 = ((bf16[64,29,2,128]{3,2,1,0:T(2,128)(2,1)}), bf16[64,29,2,128]{3,2,1,0:T(2,128)(2,1)S(1)}, u32[]{:S(2)}, u32[]{:S(2)}) async-start(bf16[64,29,2,128]{3,2,1,0:T(2,128)(2,1)} %bitcast.2), calls=%async_computation.2 | async-start | bytes 1900544 | tf_op jit(solution)/shard_map/all_to_all | solution.py:332
  91.1 1.4 copy-start.1
  142.9 12.9 %all-to-all-start.3 = ((f32[16,8,128]{2,1,0:T(8,128)}), f32[16,8,128]{2,1,0:T(8,128)S(1)}, u32[]{:S(2)}, u32[]{:S(2)}) async-start(f32[16,8,128]{2,1,0:T(8,128)} %shard_map.126), calls=%async_computation.3 | async-start | bytes 131072 | tf_op jit(solution)/shard_map/all_to_all | solution.py:332

commit v5 on v4

--- a/solution.py
+++ b/solution.py
@@ -64,7 +64,7 @@
         data[here, :] = data[here, :] + note.astype(jnp.float32)
         return s, end
 
-    lax.fori_loop(0, tiles, move, (jnp.int32(0), ints[0, 2 * tiles]), unroll=4)
+    lax.fori_loop(0, tiles, move, (jnp.int32(0), ints[0, 2 * tiles]), unroll=16)
     send_ref[...] = data[...].astype(jnp.bfloat16)
 
 
@@ -233,7 +233,7 @@
                     toks[cb, pl.ds((r * peers + b * 8) * POS + p, 8, stride=POS), :] = x + scale_ref[:, ch] * m
             return c
 
-        lax.fori_loop(0, peers // 8, body, 0)
+        lax.fori_loop(0, peers // 8, body, 0, unroll=8)
 
     def put(s, c):
         at = pl.ds(pl.multiple_of(off_ref[s] * POS, POS), POS)
@@ -241,7 +241,7 @@
             data[cb, at, :] = toks[cb, pl.ds(pl.multiple_of(s * POS, POS), POS), :]
         return c
 
-    lax.fori_loop(0, slots, put, 0, unroll=8)
+    lax.fori_loop(0, slots, put, 0, unroll=32)
     for cb in range(cbs):
         vis_ref[:, cb * LANES : (cb + 1) * LANES] = data[cb, 0 : vis_ref.shape[0], :].astype(jnp.bfloat16)
 
@@ -270,7 +270,7 @@
             rows[cb, pl.ds(pl.multiple_of(t * POS, POS), POS), :] = data[pl.ds(at, POS), :]
         return c
 
-    lax.fori_loop(0, tiles, move, 0, unroll=8)
+    lax.fori_loop(0, tiles, move, 0, unroll=32)
     for cb in range(cbs):
         out_ref[:, cb * LANES : (cb + 1) * LANES] = rows[cb].astype(jnp.bfloat16)
 
@@ -388,7 +388,6 @@
         ],
         VMEM,
     )(off, sums, data, f, gain, shift, scale)
-    back, vis = lax.optimization_barrier((back, vis))
     mine = call(functools.partial(total_kernel, meta, each), [VMEM], shape((near, 8, LANES), f32), [], VMEM)(back)
     parts = swap(mine, NEAR)
     tile_grads = call(

time: 157 us -> 156 us (level)
  blocking collectives: 9.31 us -> 65.8 us
  waiting for transfers between devices: 97.7 us -> 47.9 us
  starting transfers between devices: 29.2 us -> 23.2 us
  Pallas kernels: 15.1 us -> 13 us
    all_to_all x1 -> x2, blocking collectives: 9.31 us -> 65.8 us  [swap(): return lax.all_to_all(v, axes, split_axis=0, concat_axis=0, tiled=True)]
    all_to_all x3 -> x2, waiting for transfers between devices: 97.7 us -> 47.9 us  [swap(): return lax.all_to_all(v, axes, split_axis=0, concat_axis=0, tiled=True)]
    all_to_all x3 -> x2, starting transfers between devices: 29.2 us -> 23.2 us  [swap(): return lax.all_to_all(v, axes, split_axis=0, concat_axis=0, tiled=True)]
  transfers between devices with their start and end apart: 3 -> 2, of which waited for: 3 -> 2; matrix products, arithmetic and copies ran while one was open for 1% -> 1% of each run, Pallas kernels for 3% -> 2%
where the time goes in v5:
time: 156 us; the launch traced here: 155 us
  blocking collectives  65.8 us (42%)
  waiting for transfers between devices  47.9 us (31%)
  starting transfers between devices  23.2 us (15%)
  Pallas kernels  13 us (8%)
  local copies, waits for them, and re-layouts  3.56 us (2%)
    all_to_all x2, blocking collectives, swap(): return lax.all_to_all(v, axes, split_axis=0, concat_axis=0, tiled=True)  65.8 us
    all_to_all x2, waiting for transfers between devices, swap(): return lax.all_to_all(v, axes, split_axis=0, concat_axis=0, tiled=True)  47.9 us
    all_to_all x2, starting transfers between devices, swap(): return lax.all_to_all(v, axes, split_axis=0, concat_axis=0, tiled=True)  23.2 us
    pallas_call x1, Pallas kernels, per_device(): call(functools.partial(grad_kernel, peers, near, cap, part, each, width),...  3.21 us
  transfers between devices with their start and end apart: 2, of which 2 were waited for; matrix products, arithmetic and copies ran while one was open for 1% of the time, Pallas kernels for 2%

profile of v5, /device:TPU:2, one launch (start us, length us, event | category | flops | bytes accessed | tf_op | source)
XLA Modules:
  0.0 155.1 jit_solution(4440372513017136706)
XLA Ops:
  0.6 0.0 copy-start.4
  0.6 0.0 copy-start.5
  0.7 0.0 copy-start.6
  0.7 0.0 copy-start.3
  0.7 0.0 copy-start.2
  0.7 1.2 reshape.36.tiles_ref
  1.9 0.8 pad_add_fusion.ints_hbm
  2.7 2.1 %shard_map.121 = (bf16[3200,128]{1,0:T(8,128)(2,1)}, s32[64]{0:T(128)S(1)}) custom-call(s32[1,136]{1,0:T(1,128)S(1)} %pad_add_fusion.ints_hbm, bf16[512,384]{1,0:T(8,128)(2,1)S(1)} %reshape.36.tiles_ref), custom_call_target="tpu_custom_call" | custom-call | tf_op jit(solution)/shard_map/pallas_call | solution.py:336
  4.8 18.7 %all-to-all-start = ((bf16[64,25,2,128]{3,2,1,0:T(2,128)(2,1)}), bf16[64,25,2,128]{3,2,1,0:T(2,128)(2,1)S(1)}, u32[]{:S(2)}, u32[]{:S(2)}) async-start(bf16[64,25,2,128]{3,2,1,0:T(2,128)(2,1)} %bitcast), calls=%async_computation | async-start | bytes 1638400 | tf_op jit(solution)/shard_map/all_to_all | solution.py:332
  23.5 0.0 copy-done.4
  23.5 0.0 copy-done.5
  23.6 0.0 copy-done.6
  23.6 45.4 %all-to-all-done = bf16[64,25,2,128]{3,2,1,0:T(2,128)(2,1)S(1)} async-done(((bf16[64,25,2,128]{3,2,1,0:T(2,128)(2,1)}), bf16[64,25,2,128]{3,2,1,0:T(2,128)(2,1)S(1)}, u32[]{:S(2)}, u32[]{:S(2)}) %all-to-all-start) | async-done | bytes 819232 | tf_op jit(solution)/shard_map/all_to_all | solution.py:332
  69.0 0.0 copy-done.3
  69.0 0.0 copy-done.2
  69.0 2.6 %shard_map.122 = (f32[3200,128]{1,0:T(8,128)S(1)}, f32[3,1024,128]{2,1,0:T(8,128)S(1)}, f32[3,8,128,128]{3,2,1,0:T(8,128)S(1)}, f32[8,32,128]{2,1,0:T(8,128)S(1)}, s32[128]{0:T(128)S(1)}) custom-call(bf16[3200,128]{1,0:T(8,128)(2,1)S(1)} %bitcast.7, bf16[1024,384]{1,0:T(8,128)(2,1)S(1)} %copy-done.2, f32[49,384]{1,0:T(8,128)S(1)} %copy-done.3, ...), custom_call_target="tpu_custom_call" | custom-call | tf_op jit(solution)/shard_map/pallas_call | solution.py:345
  71.6 0.0 copy-start
  71.6 9.3 %all_to_all.20.sums_ref = f32[8,32,128]{2,1,0:T(8,128)S(1)} all-to-all(f32[8,32,128]{2,1,0:T(8,128)S(1)} %get-tuple-element.12), channel_id=1, replica_groups=mesh['zh'=4,'zl'=4,'y'=4,'x'=4,'core'=2] {'x','core'}, dimensions={0} | all-to-all | bytes 262144 | tf_op jit(solution)/shard_map/all_to_all | solution.py:332
  80.9 3.2 %shard_map.124 = bf16[3712,128]{1,0:T(8,128)(2,1)S(1)} custom-call(f32[8,32,128]{2,1,0:T(8,128)S(1)} %all_to_all.20.sums_ref, f32[3200,128]{1,0:T(8,128)S(1)} %get-tuple-element.13.data_ref, f32[3,1024,128]{2,1,0:T(8,128)S(1)} %get-tuple-element.16.ups_ref, f32[3,8,128,128]{3,2,1,0:T(8,128)S(1)} %get-tuple-element.14.f_ref, f32[49,384]{1,0:T(8,128)S(1)} %copy-done.3, ...), custom_call_target="tpu_custom_call" | custom-call | tf_op jit(solution)/shard_map/pallas_call | solution.py:367
  84.2 0.0 copy-done
  84.2 0.0 copy-start.7
  84.2 56.5 %all_to_all.21 = bf16[64,29,2,128]{3,2,1,0:T(2,128)(2,1)S(1)} all-to-all(bf16[64,29,2,128]{3,2,1,0:T(2,128)(2,1)S(1)} %bitcast.6), channel_id=1, replica_groups=mesh['zh'=4,'zl'=4,'y'=4,'x'=4,'core'=2] {'zh','zl','y'}, dimensions={0} | all-to-all | bytes 1900544 | tf_op jit(solution)/shard_map/all_to_all | solution.py:332
  140.7 0.9 shard_map.126
  141.6 4.4 %all-to-all-start.3 = ((f32[16,8,128]{2,1,0:T(8,128)}), f32[16,8,128]{2,1,0:T(8,128)S(1)}, u32[]{:S(2)}, u32[]{:S(2)}) async-start(f32[16,8,128]{2,1,0:T(8,128)} %shard_map.126), calls=%async_computation.3 | async-start | bytes 131072 | tf_op jit(solution)/shard_map/all_to_all | solution.py:332
  146.1 0.0 copy-done.7
  146.1 0.0 copy-start.1
  146.1 1.4 copy-done.1
  147.5 2.4 %shard_map.123 = bf16[1024,384]{1,0:T(8,128)(2,1)} custom-call(s32[128]{0:T(128)S(1)} %get-tuple-element.11.off_ref, f32[8,32,128]{2,1,0:T(8,128)S(1)} %all_to_all.20.sums_ref, f32[3200,128]{1,0:T(8,128)S(1)} %get-tuple-element.13.data_ref, f32[3,8,128,128]{3,2,1,0:T(8,128)S(1)} %copy-done.1, f32[1,384]{1,0:T(1,128)S(1)} %reshape.40.gain_ref, ...), custom_call_target="tpu_custom_call" | custom-call | tf_op jit(solution)/shard_map/pallas_call | solution.py:380
  149.9 1.1 shard_map.125
  151.0 0.9 reshape.45
  151.9 2.5 %all-to-all-done.3.parts_ref = f32[16,8,128]{2,1,0:T(8,128)S(1)} async-done(((f32[16,8,128]{2,1,0:T(8,128)}), f32[16,8,128]{2,1,0:T(8,128)S(1)}, u32[]{:S(2)}, u32[]{:S(2)}) %all-to-all-start.3) | async-done | bytes 65568 | tf_op jit(solution)/shard_map/all_to_all | solution.py:332
  154.5 0.7 shard_map.127
  (4 shorter events, 0.0 us)
Async XLA Ops:
  0.6 22.9 %copy-start.4 = (f32[384]{0:T(512)S(1)}, f32[384]{0:T(512)}, u32[]{:S(2)}) copy-start(f32[384]{0:T(512)} %param.13) | copy-start | bytes 4612
  0.6 22.9 %copy-start.5 = (f32[384]{0:T(512)S(1)}, f32[384]{0:T(512)}, u32[]{:S(2)}) copy-start(f32[384]{0:T(512)} %param.15) | copy-start | bytes 4612
  0.7 22.9 %copy-start.6 = (f32[384]{0:T(512)S(1)}, f32[384]{0:T(512)}, u32[]{:S(2)}) copy-start(f32[384]{0:T(512)} %param.12) | copy-start | bytes 4612
  0.7 68.3 %copy-start.3 = (f32[49,384]{1,0:T(8,128)S(1)}, f32[49,384]{1,0:T(8,128)}, u32[]{:S(2)}) copy-start(f32[49,384]{1,0:T(8,128)} %kern_ref.3) | copy-start | bytes 225796
  0.7 68.3 %copy-start.2 = (bf16[1024,384]{1,0:T(8,128)(2,1)S(1)}, bf16[1024,384]{1,0:T(8,128)(2,1)}, u32[]{:S(2)}) copy-start(bf16[1024,384]{1,0:T(8,128)(2,1)} %seq_ref.1) | copy-start | bytes 2359300
  4.8 64.2 %all-to-all-start = ((bf16[64,25,2,128]{3,2,1,0:T(2,128)(2,1)}), bf16[64,25,2,128]{3,2,1,0:T(2,128)(2,1)S(1)}, u32[]{:S(2)}, u32[]{:S(2)}) async-start(bf16[64,25,2,128]{3,2,1,0:T(2,128)(2,1)} %bitcast), calls=%async_computation | async-start | bytes 1638400 | tf_op jit(solution)/shard_map/all_to_all | solution.py:332
  71.6 12.5 %copy-start = (f32[3,8,128,128]{3,2,1,0:T(8,128)}, f32[3,8,128,128]{3,2,1,0:T(8,128)S(1)}, u32[]{:S(2)}) copy-start(f32[3,8,128,128]{3,2,1,0:T(8,128)S(1)} %get-tuple-element.14.f_ref) | copy-start | bytes 4718596
  84.2 61.9 %copy-start.7 = (f32[384]{0:T(512)S(1)}, f32[384]{0:T(512)}, u32[]{:S(2)}) copy-start(f32[384]{0:T(512)} %param.14) | copy-start | bytes 4612
  141.6 12.9 %all-to-all-start.3 = ((f32[16,8,128]{2,1,0:T(8,128)}), f32[16,8,128]{2,1,0:T(8,128)S(1)}, u32[]{:S(2)}, u32[]{:S(2)}) async-start(f32[16,8,128]{2,1,0:T(8,128)} %shard_map.126), calls=%async_computation.3 | async-start | bytes 131072 | tf_op jit(solution)/shard_map/all_to_all | solution.py:332
  146.1 1.4 copy-start.1

commit v6 on v5

--- a/solution.py
+++ b/solution.py
@@ -69,10 +69,12 @@
 
 
 def conv_kernel(peers, cap, part, got_ref, seq_ref, kern_ref, bias_ref, gain_ref, scale_ref,
-                data, ups, f_ref, sums_ref, off_ref, seq, cols, off_v, wgt_v, off_s, wgt_s, sem):
+                data, ups, f_ref, sums_ref, off_ref, both, seq, cols, off_v, wgt_v, off_s, wgt_s, sem):
     cbs = seq.shape[0]
     blocks = seq.shape[1] // POS - 1
     meta = cbs * cap * POS
+    both[0:1, :] = (scale_ref[...] * gain_ref[...]).reshape(1, -1)
+    both[1:2, :] = bias_ref[...].reshape(1, -1)
     data[...] = got_ref[...].astype(jnp.float32)
     notes = data[pl.ds(meta, peers, stride=part), :]
     notes = jnp.concatenate([notes, jnp.zeros((LANES - peers, LANES), jnp.float32)], 0).T
@@ -113,12 +115,12 @@
                 tot = [None] * 4
                 for cb in range(cbs):
                     ch = slice(cb * LANES, (cb + 1) * LANES)
-                    f = bias_ref[:, ch] + kern_ref[full(p, 0) : full(p, 0) + 1, ch] * xs[cb, 0]
+                    f = both[1:2, ch] + kern_ref[full(p, 0) : full(p, 0) + 1, ch] * xs[cb, 0]
                     for q in range(1, POS):
                         f = f + kern_ref[full(p, q) : full(p, q) + 1, ch] * xs[cb, q]
                     f_ref[cb, p, here, :] = f
                     u = ups[cb, pl.ds((r * peers + b * 8) * POS + p, 8, stride=POS), :]
-                    dn = u * (scale_ref[:, ch] * gain_ref[:, ch])
+                    dn = u * both[0:1, ch]
                     new = [f, f * f, dn, dn * f]
                     tot = new if cb == 0 else [a + n for a, n in zip(tot, new)]
                 for k in range(4):
@@ -148,11 +150,12 @@
 
 
 def grad_kernel(peers, near, cap, part, each, width, sums_ref, data_ref, ups_ref, f_ref, kern_ref, gain_ref, scale_ref,
-                out_ref, stats, data, acc, partial):
+                out_ref, both, stats, data, acc, partial):
     cbs = f_ref.shape[0]
     meta = cbs * cap * POS
     back = meta + 2 * each
     stats[...] = stats_columns(sums_ref, width)
+    both[0:1, :] = (scale_ref[...] * gain_ref[...]).reshape(1, -1)
     acc[...] = jnp.zeros_like(acc)
     for r in range(cap):
 
@@ -172,7 +175,7 @@
                     u = ups_ref[cb, pl.ds((r * peers + b * 8) * POS + p, 8, stride=POS), :]
                     f = f_ref[cb, p, here, :]
                     w = u * col[1]
-                    d = w * (scale_ref[:, ch] * gain_ref[:, ch]) + (f * col[3] + col[2])
+                    d = w * both[0:1, ch] + (f * col[3] + col[2])
                     along = w * (f - col[0])
                     df.append(d)
                     us.append(u)
@@ -228,9 +231,9 @@
                 ch = slice(cb * LANES, (cb + 1) * LANES)
                 for p in range(POS):
                     n = (f_ref[cb, p, here, :] - st[:, p : p + 1]) * st[:, POS + p : POS + p + 1]
-                    m = n * gain_ref[:, ch] + shift_ref[:, ch]
+                    m = n * gain_ref[ch] + shift_ref[ch]
                     x = data_ref[pl.ds(b * 8 * part + cb * cap * POS + r * POS + p, 8, stride=part), :]
-                    toks[cb, pl.ds((r * peers + b * 8) * POS + p, 8, stride=POS), :] = x + scale_ref[:, ch] * m
+                    toks[cb, pl.ds((r * peers + b * 8) * POS + p, 8, stride=POS), :] = x + scale_ref[ch] * m
             return c
 
         lax.fori_loop(0, peers // 8, body, 0, unroll=8)
@@ -290,9 +293,9 @@
             out_ref[tap : tap + 1, ch] = total(i)
         along, plain = total(n + 1), total(n + 2)
         out_ref[taps : taps + 1, ch] = total(n)
-        out_ref[taps + 1 : taps + 2, ch] = along * scale_ref[:, ch]
-        out_ref[taps + 2 : taps + 3, ch] = plain * scale_ref[:, ch]
-        out_ref[taps + 3 : taps + 4, ch] = along * gain_ref[:, ch] + plain * shift_ref[:, ch]
+        out_ref[taps + 1 : taps + 2, ch] = along * scale_ref[ch]
+        out_ref[taps + 2 : taps + 3, ch] = plain * scale_ref[ch]
+        out_ref[taps + 3 : taps + 4, ch] = along * gain_ref[ch] + plain * shift_ref[ch]
 
 
 ANY = pl.BlockSpec(memory_space=pl.ANY)
@@ -326,7 +329,7 @@
     part, back_part = meta + 2, meta + 2 * each
     f32, i32, bf16 = jnp.float32, jnp.int32, jnp.bfloat16
     shape = jax.ShapeDtypeStruct
-    bias, gain, shift, scale = (v.reshape(1, chans) for v in (dw_bias, ln_gain, ln_shift, layer_scale))
+    bias, gain, shift, scale = dw_bias, ln_gain, ln_shift, layer_scale
 
     def swap(v, axes):
         return lax.all_to_all(v, axes, split_axis=0, concat_axis=0, tiled=True)
@@ -353,6 +356,7 @@
             shape((slots,), i32),
         ),
         [
+            pltpu.VMEM((8, chans), f32),
             pltpu.VMEM((cbs, (blocks + 1) * POS, LANES), f32),
             pltpu.VMEM((slots, LANES), f32),
             pltpu.VMEM((8, LANES), i32),
@@ -369,6 +373,7 @@
         [VMEM] * 7,
         shape((peers * back_part, LANES), bf16),
         [
+            pltpu.VMEM((8, chans), f32),
             pltpu.VMEM((slots, LANES), f32),
             pltpu.VMEM((peers * back_part, LANES), f32),
             pltpu.VMEM((ROWS, 8, chans), f32),

time: 156 us -> 155 us (level)
  blocking collectives: 65.8 us -> 130 us
  waiting for transfers between devices: 47.9 us -> 2.56 us
  starting transfers between devices: 23.2 us -> 4.44 us
    all_to_all x2 -> x3, blocking collectives: 65.8 us -> 130 us  [swap(): return lax.all_to_all(v, axes, split_axis=0, concat_axis=0, tiled=True)]
    all_to_all x2 -> x1, waiting for transfers between devices: 47.9 us -> 2.56 us  [swap(): return lax.all_to_all(v, axes, split_axis=0, concat_axis=0, tiled=True)]
    all_to_all x2 -> x1, starting transfers between devices: 23.2 us -> 4.44 us  [swap(): return lax.all_to_all(v, axes, split_axis=0, concat_axis=0, tiled=True)]
  transfers between devices with their start and end apart: 2 -> 1, of which waited for: 2 -> 1; matrix products, arithmetic and copies ran while one was open for 1% -> 1% of each run, Pallas kernels for 2% -> 2%
where the time goes in v6:
time: 155 us; the launch traced here: 154 us
  blocking collectives  130 us (84%)
  Pallas kernels  12.6 us (8%)
  starting transfers between devices  4.44 us (3%)
  local copies, waits for them, and re-layouts  3.55 us (2%)
  waiting for transfers between devices  2.56 us (2%)
    all_to_all x3, blocking collectives, swap(): return lax.all_to_all(v, axes, split_axis=0, concat_axis=0, tiled=True)  130 us
    all_to_all x1, starting transfers between devices, swap(): return lax.all_to_all(v, axes, split_axis=0, concat_axis=0, tiled=True)  4.44 us
    pallas_call x1, Pallas kernels, per_device(): call(functools.partial(grad_kernel, peers, near, cap, part, each, width),...  3.23 us
  transfers between devices with their start and end apart: 1, of which 1 were waited for; matrix products, arithmetic and copies ran while one was open for 1% of the time, Pallas kernels for 2%

profile of v6, /device:TPU:2, one launch (start us, length us, event | category | flops | bytes accessed | tf_op | source)
XLA Modules:
  0.0 154.5 jit_solution(9761274117579112091)
XLA Ops:
  0.6 0.0 copy-start.5
  0.6 0.0 copy-start.4
  0.7 0.0 copy-start.3
  0.7 0.0 copy-start.2
  0.7 0.0 copy-start.7
  0.7 1.2 reshape.24.tiles_ref
  1.9 0.8 pad_add_fusion.ints_hbm
  2.7 1.7 %shard_map.121 = (bf16[3200,128]{1,0:T(8,128)(2,1)S(1)}, s32[64]{0:T(128)S(1)}) custom-call(s32[1,136]{1,0:T(1,128)S(1)} %pad_add_fusion.ints_hbm, bf16[512,384]{1,0:T(8,128)(2,1)S(1)} %reshape.24.tiles_ref), custom_call_target="tpu_custom_call" | custom-call | tf_op jit(solution)/shard_map/pallas_call | solution.py:339
  4.3 64.0 %all_to_all.20 = bf16[64,25,2,128]{3,2,1,0:T(2,128)(2,1)S(1)} all-to-all(bf16[64,25,2,128]{3,2,1,0:T(2,128)(2,1)S(1)} %bitcast.8), channel_id=1, replica_groups=mesh['zh'=4,'zl'=4,'y'=4,'x'=4,'core'=2] {'zh','zl','y'}, dimensions={0} | all-to-all | bytes 1638400 | tf_op jit(solution)/shard_map/all_to_all | solution.py:335
  68.3 0.0 copy-done.5
  68.3 0.0 copy-done.4
  68.3 0.0 copy-done.3
  68.3 0.0 copy-done.2
  68.4 0.0 copy-done.7
  68.4 2.6 %shard_map.122 = (f32[3200,128]{1,0:T(8,128)S(1)}, f32[3,1024,128]{2,1,0:T(8,128)S(1)}, f32[3,8,128,128]{3,2,1,0:T(8,128)S(1)}, f32[8,32,128]{2,1,0:T(8,128)S(1)}, s32[128]{0:T(128)S(1)}) custom-call(bf16[3200,128]{1,0:T(8,128)(2,1)S(1)} %bitcast.7, bf16[1024,384]{1,0:T(8,128)(2,1)S(1)} %copy-done.2, f32[49,384]{1,0:T(8,128)S(1)} %copy-done.3, ...), custom_call_target="tpu_custom_call" | custom-call | tf_op jit(solution)/shard_map/pallas_call | solution.py:348
  71.0 0.0 copy-start
  71.0 9.3 %all_to_all.21.sums_ref = f32[8,32,128]{2,1,0:T(8,128)S(1)} all-to-all(f32[8,32,128]{2,1,0:T(8,128)S(1)} %get-tuple-element.12), channel_id=1, replica_groups=mesh['zh'=4,'zl'=4,'y'=4,'x'=4,'core'=2] {'x','core'}, dimensions={0} | all-to-all | bytes 262144 | tf_op jit(solution)/shard_map/all_to_all | solution.py:335
  80.3 3.2 %shard_map.124 = bf16[3712,128]{1,0:T(8,128)(2,1)S(1)} custom-call(f32[8,32,128]{2,1,0:T(8,128)S(1)} %all_to_all.21.sums_ref, f32[3200,128]{1,0:T(8,128)S(1)} %get-tuple-element.13.data_ref, f32[3,1024,128]{2,1,0:T(8,128)S(1)} %get-tuple-element.16.ups_ref, f32[3,8,128,128]{3,2,1,0:T(8,128)S(1)} %get-tuple-element.14.f_ref, f32[49,384]{1,0:T(8,128)S(1)} %copy-done.3, ...), custom_call_target="tpu_custom_call" | custom-call | tf_op jit(solution)/shard_map/pallas_call | solution.py:371
  83.5 0.0 copy-done
  83.6 0.0 copy-start.6
  83.6 56.5 %all_to_all.22 = bf16[64,29,2,128]{3,2,1,0:T(2,128)(2,1)S(1)} all-to-all(bf16[64,29,2,128]{3,2,1,0:T(2,128)(2,1)S(1)} %bitcast.6), channel_id=1, replica_groups=mesh['zh'=4,'zl'=4,'y'=4,'x'=4,'core'=2] {'zh','zl','y'}, dimensions={0} | all-to-all | bytes 1900544 | tf_op jit(solution)/shard_map/all_to_all | solution.py:335
  140.1 0.9 shard_map.126
  141.0 4.4 %all-to-all-start.3 = ((f32[16,8,128]{2,1,0:T(8,128)}), f32[16,8,128]{2,1,0:T(8,128)S(1)}, u32[]{:S(2)}, u32[]{:S(2)}) async-start(f32[16,8,128]{2,1,0:T(8,128)} %shard_map.126), calls=%async_computation.3 | async-start | bytes 131072 | tf_op jit(solution)/shard_map/all_to_all | solution.py:335
  145.4 0.0 copy-done.6
  145.4 0.0 copy-start.1
  145.4 1.4 copy-done.1
  146.8 2.4 %shard_map.123 = bf16[1024,384]{1,0:T(8,128)(2,1)} custom-call(s32[128]{0:T(128)S(1)} %get-tuple-element.11.off_ref, f32[8,32,128]{2,1,0:T(8,128)S(1)} %all_to_all.21.sums_ref, f32[3200,128]{1,0:T(8,128)S(1)} %get-tuple-element.13.data_ref, f32[3,8,128,128]{3,2,1,0:T(8,128)S(1)} %copy-done.1, f32[384]{0:T(512)S(1)} %copy-done.4, f32[384]{0:T(512)S(1)} %copy-done.6, ...), custom_call_target="tpu_custom_call" | custom-call | tf_op jit(solution)/shard_map/pallas_call | solution.py:385
  149.3 1.1 shard_map.125
  150.4 0.9 reshape.29
  151.3 2.6 %all-to-all-done.3.parts_ref = f32[16,8,128]{2,1,0:T(8,128)S(1)} async-done(((f32[16,8,128]{2,1,0:T(8,128)}), f32[16,8,128]{2,1,0:T(8,128)S(1)}, u32[]{:S(2)}, u32[]{:S(2)}) %all-to-all-start.3) | async-done | bytes 65568 | tf_op jit(solution)/shard_map/all_to_all | solution.py:335
  153.8 0.7 shard_map.127
Async XLA Ops:
  0.6 67.7 %copy-start.5 = (f32[384]{0:T(512)S(1)}, f32[384]{0:T(512)}, u32[]{:S(2)}) copy-start(f32[384]{0:T(512)} %scale_ref.7) | copy-start | bytes 4612
  0.6 67.7 %copy-start.4 = (f32[384]{0:T(512)S(1)}, f32[384]{0:T(512)}, u32[]{:S(2)}) copy-start(f32[384]{0:T(512)} %gain_ref.7) | copy-start | bytes 4612
  0.7 67.7 %copy-start.3 = (f32[49,384]{1,0:T(8,128)S(1)}, f32[49,384]{1,0:T(8,128)}, u32[]{:S(2)}) copy-start(f32[49,384]{1,0:T(8,128)} %kern_ref.3) | copy-start | bytes 225796
  0.7 67.7 %copy-start.2 = (bf16[1024,384]{1,0:T(8,128)(2,1)S(1)}, bf16[1024,384]{1,0:T(8,128)(2,1)}, u32[]{:S(2)}) copy-start(bf16[1024,384]{1,0:T(8,128)(2,1)} %seq_ref.1) | copy-start | bytes 2359300
  0.7 67.7 %copy-start.7 = (f32[384]{0:T(512)S(1)}, f32[384]{0:T(512)}, u32[]{:S(2)}) copy-start(f32[384]{0:T(512)} %bias_ref.1) | copy-start | bytes 4612
  71.0 12.6 %copy-start = (f32[3,8,128,128]{3,2,1,0:T(8,128)}, f32[3,8,128,128]{3,2,1,0:T(8,128)S(1)}, u32[]{:S(2)}) copy-start(f32[3,8,128,128]{3,2,1,0:T(8,128)S(1)} %get-tuple-element.14.f_ref) | copy-start | bytes 4718596
  83.6 61.9 %copy-start.6 = (f32[384]{0:T(512)S(1)}, f32[384]{0:T(512)}, u32[]{:S(2)}) copy-start(f32[384]{0:T(512)} %shift_ref.3) | copy-start | bytes 4612
  141.0 12.9 %all-to-all-start.3 = ((f32[16,8,128]{2,1,0:T(8,128)}), f32[16,8,128]{2,1,0:T(8,128)S(1)}, u32[]{:S(2)}, u32[]{:S(2)}) async-start(f32[16,8,128]{2,1,0:T(8,128)} %shard_map.126), calls=%async_computation.3 | async-start | bytes 131072 | tf_op jit(solution)/shard_map/all_to_all | solution.py:335
  145.4 1.4 copy-start.1
